TPU v7x, 32 devices: a whole 2x2x4 slice. The times are simulated.
32 devices in a mesh: row: 8 (over z, x), col: 4 (over y, core).
Axes of the slice: x: 2, y: 2, z: 4, core: 2. Of those that a mesh axis runs over, the one named last changes fastest.
Arguments:
- estimate: float32 [8, 256, 512], P(None, 'row', 'col'), may hold values from 0.5 to 2
- views_data: bfloat16 [4, 8, 256, 512], P(None, None, 'row', 'col'), may hold values from 0.25 to 4
- psf_rows: float32 [4, 33], replicated, may hold values from 0.05 to 1
- psf_cols: float32 [4, 33], replicated, may hold values from 0.05 to 1
Outputs:
- estimate_next: float32 [8, 256, 512], P(None, 'row', 'col')
All inputs are finite; a program needn't handle non-finite values.
Results may differ from a plain program's by a relative error of at most 0.0003.
Values may be sent and summed in bfloat16 or wider, within the bound.
A program may use at most 64 MiB of HBM per device.

v0:
```python
import jax
import jax.numpy as jnp
from jax import lax
from jax.sharding import PartitionSpec as P


def extended_2(shard, sides, width):
    for axis, dim in sides:
        size, length = (lax.axis_size(axis), shard.shape[dim])
        up = [(i, (i + 1) % size) for i in range(size - 1)]
        down = [(j, i) for i, j in up]
        last = lax.slice_in_dim(shard, length - width, length, axis=dim)
        leading = lax.slice_in_dim(shard, 0, width, axis=dim)
        before = lax.ppermute(last, axis, up)
        after = lax.ppermute(leading, axis, down)
        shard = jnp.concatenate([before, shard, after], axis=dim)
    return shard


def band_matrix(kernel, out_len, mirrored):
    taps = kernel.shape[0]
    row_index = lax.broadcasted_iota(jnp.int32, (out_len, out_len + taps - 1), 0)
    col_index = lax.broadcasted_iota(jnp.int32, (out_len, out_len + taps - 1), 1)
    offset = col_index - row_index
    if mirrored:
        offset = taps - 1 - offset
    tap_index = jnp.arange(taps, dtype=jnp.int32)
    matches = (offset[:, :, None] == tap_index[None, None, :]).astype(jnp.float32)
    return jnp.einsum("ijt,t->ij", matches, kernel, precision=lax.Precision.HIGHEST)


def blur_block(padded, kernel_y, kernel_x, mirrored):
    taps = kernel_y.shape[0]
    out_y = padded.shape[1] - (taps - 1)
    out_x = padded.shape[2] - (taps - 1)
    band_x = band_matrix(kernel_x, out_x, mirrored)
    band_y = band_matrix(kernel_y, out_y, mirrored)
    across = jnp.einsum("zyj,xj->zyx", padded, band_x, precision=lax.Precision.HIGHEST)
    return jnp.einsum("zjx,yj->zyx", across, band_y, precision=lax.Precision.HIGHEST)


def rim_estimate(estimate, reach):
    return extended_2(estimate.astype(jnp.bfloat16), (("row", 1), ("col", 2)), reach).astype(
        estimate.dtype
    )


def local(estimate, views_data, psf_rows, psf_cols):
    reach = (psf_rows.shape[1] - 1) // 2
    view_count = views_data.shape[0]
    kernels_y = psf_rows / jnp.sum(psf_rows, axis=1, keepdims=True)
    kernels_x = psf_cols / jnp.sum(psf_cols, axis=1, keepdims=True)
    log_sum = jnp.zeros(estimate.shape, jnp.float32)
    padded = rim_estimate(estimate, reach)
    quotients = []
    for view_index in range(view_count):
        blurred = blur_block(padded, kernels_y[view_index], kernels_x[view_index], False)
        quotients.append(views_data[view_index].astype(jnp.float32) / blurred)
    for view_index in range(view_count):
        extended = extended_2(
            quotients[view_index].astype(jnp.bfloat16), (("row", 1), ("col", 2)), reach
        ).astype(jnp.float32)
        correction = blur_block(extended, kernels_y[view_index], kernels_x[view_index], True)
        log_sum = log_sum + jnp.log(correction)
    return estimate * jnp.exp(log_sum / view_count)


def solution(mesh):
    return jax.shard_map(
        local,
        mesh=mesh,
        in_specs=(P(None, "row", "col"), P(None, None, "row", "col"), P(), P()),
        out_specs=P(None, "row", "col"),
        check_vma=False,
    )
```

profile of v0, /device:TPU:9, one launch (start us, length us, event | category | flops | bytes accessed | tf_op | source)
XLA Modules:
  0.0 94.3 jit_solution(759998229274680382)
XLA Ops:
  0.9 3.1 %collective-permute-start = (bf16[8,16,128]{2,1,0:T(8,128)(2,1)S(1)}, bf16[8,16,128]{2,1,0:T(8,128)(2,1)S(1)}, u32[]{:S(2)}, u32[]{:S(2)}) collective-permute-start(bf16[8,16,128]{2,1,0:T(8,128)(2,1)S(1)} %get-tuple-element.23), channel_id=1, source_target_pairs={{0,4},{4,8},{8,12},{12,16},{16,20},{20,24},{24,28},{1,5},{5,9},{9,... | collective-permute-start | bytes 98312 | tf_op jit(solution)/shard_map/ppermute | solution.py:14
  4.1 3.1 %collective-permute-start.1 = (bf16[8,16,128]{2,1,0:T(8,128)(2,1)S(1)}, bf16[8,16,128]{2,1,0:T(8,128)(2,1)S(1)}, u32[]{:S(2)}, u32[]{:S(2)}) collective-permute-start(bf16[8,16,128]{2,1,0:T(8,128)(2,1)S(1)} %get-tuple-element.24), channel_id=1, source_target_pairs={{4,0},{8,4},{12,8},{16,12},{20,16},{24,20},{28,24},{5,1},{9,5},{13... | collective-permute-start | bytes 98312 | tf_op jit(solution)/shard_map/ppermute | solution.py:15
  8.7 1.4 %fusion.24 = f32[1,32,64]{2,0,1:T(1,128)S(1)} fusion(s32[32,64]{1,0:T(8,128)S(1)} %iota_subtract_fusion.1, f32[4,33]{1,0:T(4,128)S(1)} %broadcast_divide_fusion.1), kind=kOutput, calls=%fused_computation.37 | convolution fusion | flops 878592 | bytes 25088 | tf_op jit(solution)/shard_map/ijt,t->ij/dot_general | solution.py:29
  10.1 1.4 %fusion.25 = f32[1,32,64]{2,0,1:T(1,128)S(1)} fusion(s32[32,64]{1,0:T(8,128)S(1)} %iota_subtract_fusion.1, f32[4,33]{1,0:T(4,128)S(1)} %broadcast_divide_fusion.1), kind=kOutput, calls=%fused_computation.38 | convolution fusion | flops 878592 | bytes 25088 | tf_op jit(solution)/shard_map/ijt,t->ij/dot_general | solution.py:29
  11.5 1.4 %fusion.26 = f32[1,32,64]{2,0,1:T(1,128)S(1)} fusion(s32[32,64]{1,0:T(8,128)S(1)} %iota_subtract_fusion.1, f32[4,33]{1,0:T(4,128)S(1)} %broadcast_divide_fusion.1), kind=kOutput, calls=%fused_computation.39 | convolution fusion | flops 878592 | bytes 25088 | tf_op jit(solution)/shard_map/ijt,t->ij/dot_general | solution.py:29
  12.9 1.4 %fusion.23 = f32[1,32,64]{2,0,1:T(1,128)S(1)} fusion(s32[32,64]{1,0:T(8,128)S(1)} %iota_subtract_fusion.1, f32[4,33]{1,0:T(4,128)S(1)} %broadcast_divide_fusion.1), kind=kOutput, calls=%fused_computation.36 | convolution fusion | flops 878592 | bytes 25088 | tf_op jit(solution)/shard_map/ijt,t->ij/dot_general | solution.py:29
  14.3 1.4 %fusion.27 = f32[1,32,64]{2,0,1:T(1,128)S(1)} fusion(s32[32,64]{1,0:T(8,128)S(1)} %broadcast_subtract_fusion.1, f32[4,33]{1,0:T(4,128)S(1)} %broadcast_divide_fusion.1), kind=kOutput, calls=%fused_computation.41 | convolution fusion | flops 878592 | bytes 25088 | tf_op jit(solution)/shard_map/ijt,t->ij/dot_general | solution.py:29
  15.7 1.4 %fusion.28 = f32[1,32,64]{2,0,1:T(1,128)S(1)} fusion(s32[32,64]{1,0:T(8,128)S(1)} %broadcast_subtract_fusion.1, f32[4,33]{1,0:T(4,128)S(1)} %broadcast_divide_fusion.1), kind=kOutput, calls=%fused_computation.42 | convolution fusion | flops 878592 | bytes 25088 | tf_op jit(solution)/shard_map/ijt,t->ij/dot_general | solution.py:29
  24.7 1.1 %fusion.7 = f32[1,128,160]{1,0,2:T(1,128)S(1)} fusion(pred[128,160,33]{0,1,2:T(32,128)(4,1)S(1)} %iota_compare_fusion, f32[4,33]{1,0:T(4,128)S(1)} %broadcast_divide_fusion), kind=kOutput, calls=%fused_computation.11 | convolution fusion | flops 8785920 | bytes 758272 | tf_op jit(solution)/shard_map/ijt,t->ij/dot_general | solution.py:29
  25.9 1.4 %fusion.29 = f32[1,32,64]{2,0,1:T(1,128)S(1)} fusion(s32[32,64]{1,0:T(8,128)S(1)} %broadcast_subtract_fusion.1, f32[4,33]{1,0:T(4,128)S(1)} %broadcast_divide_fusion.1), kind=kOutput, calls=%fused_computation.43 | convolution fusion | flops 878592 | bytes 25088 | tf_op jit(solution)/shard_map/ijt,t->ij/dot_general | solution.py:29
  27.4 4.3 %collective-permute-start.2 = (bf16[8,64,16]{2,1,0:T(8,128)(2,1)S(1)}, bf16[8,64,16]{2,1,0:T(8,128)(2,1)S(1)}, u32[]{:S(2)}, u32[]{:S(2)}) collective-permute-start(bf16[8,64,16]{2,1,0:T(8,128)(2,1)S(1)} %get-tuple-element.13), channel_id=1, source_target_pairs={{0,1},{1,2},{2,3},{4,5},{5,6},{6,7},{8,9},{9,10},{10,11},{12,13},{... | collective-permute-start | bytes 49160 | tf_op jit(solution)/shard_map/ppermute | solution.py:14
  31.7 1.9 %collective-permute-start.3 = (bf16[8,64,16]{2,1,0:T(8,128)(2,1)S(1)}, bf16[8,64,16]{2,1,0:T(8,128)(2,1)S(1)}, u32[]{:S(2)}, u32[]{:S(2)}) collective-permute-start(bf16[8,64,16]{2,1,0:T(8,128)(2,1)S(1)} %get-tuple-element.14), channel_id=1, source_target_pairs={{1,0},{2,1},{3,2},{5,4},{6,5},{7,6},{9,8},{10,9},{11,10},{13,12},{... | collective-permute-start | bytes 49160 | tf_op jit(solution)/shard_map/ppermute | solution.py:15
  33.6 1.4 %fusion.30 = f32[1,32,64]{2,0,1:T(1,128)S(1)} fusion(s32[32,64]{1,0:T(8,128)S(1)} %broadcast_subtract_fusion.1, f32[4,33]{1,0:T(4,128)S(1)} %broadcast_divide_fusion.1), kind=kOutput, calls=%fused_computation.44 | convolution fusion | flops 878592 | bytes 25088 | tf_op jit(solution)/shard_map/ijt,t->ij/dot_general | solution.py:29
  35.0 3.0 %collective-permute-done.3 = bf16[8,64,16]{2,1,0:T(8,128)(2,1)S(1)} collective-permute-done((bf16[8,64,16]{2,1,0:T(8,128)(2,1)S(1)}, bf16[8,64,16]{2,1,0:T(8,128)(2,1)S(1)}, u32[]{:S(2)}, u32[]{:S(2)}) %collective-permute-start.3) | collective-permute-done | bytes 16416 | tf_op jit(solution)/shard_map/ppermute | solution.py:15
  38.8 2.2 %collective-permute-start.16 = (bf16[8,16,128]{2,1,0:T(8,128)(2,1)S(1)}, bf16[8,16,128]{2,1,0:T(8,128)(2,1)S(1)}, u32[]{:S(2)}, u32[]{:S(2)}) collective-permute-start(bf16[8,16,128]{2,1,0:T(8,128)(2,1)S(1)} %get-tuple-element.21), channel_id=1, source_target_pairs={{0,4},{4,8},{8,12},{12,16},{16,20},{20,24},{24,28},{1,5},{5,9},{9,... | collective-permute-start | bytes 98312 | tf_op jit(solution)/shard_map/ppermute | solution.py:14
  41.1 4.0 %collective-permute-start.17 = (bf16[8,16,128]{2,1,0:T(8,128)(2,1)S(1)}, bf16[8,16,128]{2,1,0:T(8,128)(2,1)S(1)}, u32[]{:S(2)}, u32[]{:S(2)}) collective-permute-start(bf16[8,16,128]{2,1,0:T(8,128)(2,1)S(1)} %get-tuple-element.22), channel_id=1, source_target_pairs={{4,0},{8,4},{12,8},{16,12},{20,16},{24,20},{28,24},{5,1},{9,5},{13... | collective-permute-start | bytes 98312 | tf_op jit(solution)/shard_map/ppermute | solution.py:15
  45.7 2.0 %collective-permute-start.4 = (bf16[8,16,128]{2,1,0:T(8,128)(2,1)S(1)}, bf16[8,16,128]{2,1,0:T(8,128)(2,1)S(1)}, u32[]{:S(2)}, u32[]{:S(2)}) collective-permute-start(bf16[8,16,128]{2,1,0:T(8,128)(2,1)S(1)} %get-tuple-element.15), channel_id=1, source_target_pairs={{0,4},{4,8},{8,12},{12,16},{16,20},{20,24},{24,28},{1,5},{5,9},{9,... | collective-permute-start | bytes 98312 | tf_op jit(solution)/shard_map/ppermute | solution.py:14
  47.7 4.1 %collective-permute-start.5 = (bf16[8,16,128]{2,1,0:T(8,128)(2,1)S(1)}, bf16[8,16,128]{2,1,0:T(8,128)(2,1)S(1)}, u32[]{:S(2)}, u32[]{:S(2)}) collective-permute-start(bf16[8,16,128]{2,1,0:T(8,128)(2,1)S(1)} %get-tuple-element.16), channel_id=1, source_target_pairs={{4,0},{8,4},{12,8},{16,12},{20,16},{24,20},{28,24},{5,1},{9,5},{13... | collective-permute-start | bytes 98312 | tf_op jit(solution)/shard_map/ppermute | solution.py:15
  52.9 2.0 %collective-permute-start.8 = (bf16[8,16,128]{2,1,0:T(8,128)(2,1)S(1)}, bf16[8,16,128]{2,1,0:T(8,128)(2,1)S(1)}, u32[]{:S(2)}, u32[]{:S(2)}) collective-permute-start(bf16[8,16,128]{2,1,0:T(8,128)(2,1)S(1)} %get-tuple-element.17), channel_id=1, source_target_pairs={{0,4},{4,8},{8,12},{12,16},{16,20},{20,24},{24,28},{1,5},{5,9},{9,... | collective-permute-start | bytes 98312 | tf_op jit(solution)/shard_map/ppermute | solution.py:14
  55.3 4.1 %collective-permute-start.9 = (bf16[8,16,128]{2,1,0:T(8,128)(2,1)S(1)}, bf16[8,16,128]{2,1,0:T(8,128)(2,1)S(1)}, u32[]{:S(2)}, u32[]{:S(2)}) collective-permute-start(bf16[8,16,128]{2,1,0:T(8,128)(2,1)S(1)} %get-tuple-element.18), channel_id=1, source_target_pairs={{4,0},{8,4},{12,8},{16,12},{20,16},{24,20},{28,24},{5,1},{9,5},{13... | collective-permute-start | bytes 98312 | tf_op jit(solution)/shard_map/ppermute | solution.py:15
  59.4 2.0 %collective-permute-start.12 = (bf16[8,16,128]{2,1,0:T(8,128)(2,1)S(1)}, bf16[8,16,128]{2,1,0:T(8,128)(2,1)S(1)}, u32[]{:S(2)}, u32[]{:S(2)}) collective-permute-start(bf16[8,16,128]{2,1,0:T(8,128)(2,1)S(1)} %get-tuple-element.19), channel_id=1, source_target_pairs={{0,4},{4,8},{8,12},{12,16},{16,20},{20,24},{24,28},{1,5},{5,9},{9,... | collective-permute-start | bytes 98312 | tf_op jit(solution)/shard_map/ppermute | solution.py:14
  61.6 4.1 %collective-permute-start.13 = (bf16[8,16,128]{2,1,0:T(8,128)(2,1)S(1)}, bf16[8,16,128]{2,1,0:T(8,128)(2,1)S(1)}, u32[]{:S(2)}, u32[]{:S(2)}) collective-permute-start(bf16[8,16,128]{2,1,0:T(8,128)(2,1)S(1)} %get-tuple-element.20), channel_id=1, source_target_pairs={{4,0},{8,4},{12,8},{16,12},{20,16},{24,20},{28,24},{5,1},{9,5},{13... | collective-permute-start | bytes 98312 | tf_op jit(solution)/shard_map/ppermute | solution.py:15
  65.8 4.0 %collective-permute-start.18 = (bf16[8,64,16]{2,1,0:T(8,128)(2,1)S(1)}, bf16[8,64,16]{2,1,0:T(8,128)(2,1)S(1)}, u32[]{:S(2)}, u32[]{:S(2)}) collective-permute-start(bf16[8,64,16]{2,1,0:T(8,128)(2,1)S(1)} %get-tuple-element.11), channel_id=1, source_target_pairs={{0,1},{1,2},{2,3},{4,5},{5,6},{6,7},{8,9},{9,10},{10,11},{12,13},{... | collective-permute-start | bytes 49160 | tf_op jit(solution)/shard_map/ppermute | solution.py:14
  69.9 1.9 %collective-permute-start.19 = (bf16[8,64,16]{2,1,0:T(8,128)(2,1)S(1)}, bf16[8,64,16]{2,1,0:T(8,128)(2,1)S(1)}, u32[]{:S(2)}, u32[]{:S(2)}) collective-permute-start(bf16[8,64,16]{2,1,0:T(8,128)(2,1)S(1)} %get-tuple-element.12), channel_id=1, source_target_pairs={{1,0},{2,1},{3,2},{5,4},{6,5},{7,6},{9,8},{10,9},{11,10},{13,12},{... | collective-permute-start | bytes 49160 | tf_op jit(solution)/shard_map/ppermute | solution.py:15
  71.9 3.6 %collective-permute-start.6 = (bf16[8,64,16]{2,1,0:T(8,128)(2,1)S(1)}, bf16[8,64,16]{2,1,0:T(8,128)(2,1)S(1)}, u32[]{:S(2)}, u32[]{:S(2)}) collective-permute-start(bf16[8,64,16]{2,1,0:T(8,128)(2,1)S(1)} %get-tuple-element.5), channel_id=1, source_target_pairs={{0,1},{1,2},{2,3},{4,5},{5,6},{6,7},{8,9},{9,10},{10,11},{12,13},{... | collective-permute-start | bytes 49160 | tf_op jit(solution)/shard_map/ppermute | solution.py:14
  75.7 1.9 %collective-permute-start.10 = (bf16[8,64,16]{2,1,0:T(8,128)(2,1)S(1)}, bf16[8,64,16]{2,1,0:T(8,128)(2,1)S(1)}, u32[]{:S(2)}, u32[]{:S(2)}) collective-permute-start(bf16[8,64,16]{2,1,0:T(8,128)(2,1)S(1)} %get-tuple-element.7), channel_id=1, source_target_pairs={{0,1},{1,2},{2,3},{4,5},{5,6},{6,7},{8,9},{9,10},{10,11},{12,13},{... | collective-permute-start | bytes 49160 | tf_op jit(solution)/shard_map/ppermute | solution.py:14
  77.6 2.4 %collective-permute-start.11 = (bf16[8,64,16]{2,1,0:T(8,128)(2,1)S(1)}, bf16[8,64,16]{2,1,0:T(8,128)(2,1)S(1)}, u32[]{:S(2)}, u32[]{:S(2)}) collective-permute-start(bf16[8,64,16]{2,1,0:T(8,128)(2,1)S(1)} %get-tuple-element.8), channel_id=1, source_target_pairs={{1,0},{2,1},{3,2},{5,4},{6,5},{7,6},{9,8},{10,9},{11,10},{13,12},{... | collective-permute-start | bytes 49160 | tf_op jit(solution)/shard_map/ppermute | solution.py:15
  80.2 3.7 %collective-permute-start.14 = (bf16[8,64,16]{2,1,0:T(8,128)(2,1)S(1)}, bf16[8,64,16]{2,1,0:T(8,128)(2,1)S(1)}, u32[]{:S(2)}, u32[]{:S(2)}) collective-permute-start(bf16[8,64,16]{2,1,0:T(8,128)(2,1)S(1)} %get-tuple-element.9), channel_id=1, source_target_pairs={{0,1},{1,2},{2,3},{4,5},{5,6},{6,7},{8,9},{9,10},{10,11},{12,13},{... | collective-permute-start | bytes 49160 | tf_op jit(solution)/shard_map/ppermute | solution.py:14
  83.9 1.9 %collective-permute-start.15 = (bf16[8,64,16]{2,1,0:T(8,128)(2,1)S(1)}, bf16[8,64,16]{2,1,0:T(8,128)(2,1)S(1)}, u32[]{:S(2)}, u32[]{:S(2)}) collective-permute-start(bf16[8,64,16]{2,1,0:T(8,128)(2,1)S(1)} %get-tuple-element.10), channel_id=1, source_target_pairs={{1,0},{2,1},{3,2},{5,4},{6,5},{7,6},{9,8},{10,9},{11,10},{13,12},{... | collective-permute-start | bytes 49160 | tf_op jit(solution)/shard_map/ppermute | solution.py:15
  86.6 1.9 %collective-permute-start.7 = (bf16[8,64,16]{2,1,0:T(8,128)(2,1)S(1)}, bf16[8,64,16]{2,1,0:T(8,128)(2,1)S(1)}, u32[]{:S(2)}, u32[]{:S(2)}) collective-permute-start(bf16[8,64,16]{2,1,0:T(8,128)(2,1)S(1)} %get-tuple-element.6), channel_id=1, source_target_pairs={{1,0},{2,1},{3,2},{5,4},{6,5},{7,6},{9,8},{10,9},{11,10},{13,12},{... | collective-permute-start | bytes 49160 | tf_op jit(solution)/shard_map/ppermute | solution.py:15
  88.5 1.7 %collective-permute-done.15 = bf16[8,64,16]{2,1,0:T(8,128)(2,1)S(1)} collective-permute-done((bf16[8,64,16]{2,1,0:T(8,128)(2,1)S(1)}, bf16[8,64,16]{2,1,0:T(8,128)(2,1)S(1)}, u32[]{:S(2)}, u32[]{:S(2)}) %collective-permute-start.15) | collective-permute-done | bytes 16416 | tf_op jit(solution)/shard_map/ppermute | solution.py:15
  91.7 1.2 %collective-permute-done.7 = bf16[8,64,16]{2,1,0:T(8,128)(2,1)S(1)} collective-permute-done((bf16[8,64,16]{2,1,0:T(8,128)(2,1)S(1)}, bf16[8,64,16]{2,1,0:T(8,128)(2,1)S(1)}, u32[]{:S(2)}, u32[]{:S(2)}) %collective-permute-start.7) | collective-permute-done | bytes 16416 | tf_op jit(solution)/shard_map/ppermute | solution.py:15
  (73 shorter events, 17.0 us)
Async XLA Ops:
  0.9 26.3 %collective-permute-start = (bf16[8,16,128]{2,1,0:T(8,128)(2,1)S(1)}, bf16[8,16,128]{2,1,0:T(8,128)(2,1)S(1)}, u32[]{:S(2)}, u32[]{:S(2)}) collective-permute-start(bf16[8,16,128]{2,1,0:T(8,128)(2,1)S(1)} %get-tuple-element.23), channel_id=1, source_target_pairs={{0,4},{4,8},{8,12},{12,16},{16,20},{20,24},{24,28},{1,5},{5,9},{9,... | collective-permute-start | bytes 98312 | tf_op jit(solution)/shard_map/ppermute | solution.py:14
  4.1 23.2 %collective-permute-start.1 = (bf16[8,16,128]{2,1,0:T(8,128)(2,1)S(1)}, bf16[8,16,128]{2,1,0:T(8,128)(2,1)S(1)}, u32[]{:S(2)}, u32[]{:S(2)}) collective-permute-start(bf16[8,16,128]{2,1,0:T(8,128)(2,1)S(1)} %get-tuple-element.24), channel_id=1, source_target_pairs={{4,0},{8,4},{12,8},{16,12},{20,16},{24,20},{28,24},{5,1},{9,5},{13... | collective-permute-start | bytes 98312 | tf_op jit(solution)/shard_map/ppermute | solution.py:15
  11.5 5.7 %copy-start.1 = (f32[4,33]{1,0:T(4,128)S(1)}, f32[4,33]{1,0:T(4,128)}, u32[]{:S(2)}) copy-start(f32[4,33]{1,0:T(4,128)} %param.7) | copy-start | bytes 1588
  27.4 7.6 %collective-permute-start.2 = (bf16[8,64,16]{2,1,0:T(8,128)(2,1)S(1)}, bf16[8,64,16]{2,1,0:T(8,128)(2,1)S(1)}, u32[]{:S(2)}, u32[]{:S(2)}) collective-permute-start(bf16[8,64,16]{2,1,0:T(8,128)(2,1)S(1)} %get-tuple-element.13), channel_id=1, source_target_pairs={{0,1},{1,2},{2,3},{4,5},{5,6},{6,7},{8,9},{9,10},{10,11},{12,13},{... | collective-permute-start | bytes 49160 | tf_op jit(solution)/shard_map/ppermute | solution.py:14
  31.7 6.3 %collective-permute-start.3 = (bf16[8,64,16]{2,1,0:T(8,128)(2,1)S(1)}, bf16[8,64,16]{2,1,0:T(8,128)(2,1)S(1)}, u32[]{:S(2)}, u32[]{:S(2)}) collective-permute-start(bf16[8,64,16]{2,1,0:T(8,128)(2,1)S(1)} %get-tuple-element.14), channel_id=1, source_target_pairs={{1,0},{2,1},{3,2},{5,4},{6,5},{7,6},{9,8},{10,9},{11,10},{13,12},{... | collective-permute-start | bytes 49160 | tf_op jit(solution)/shard_map/ppermute | solution.py:15
  35.0 3.5 %copy-start.2 = (bf16[4,8,32,128]{3,2,1,0:T(8,128)(2,1)S(1)}, bf16[4,8,32,128]{3,2,1,0:T(8,128)(2,1)}, u32[]{:S(2)}) copy-start(bf16[4,8,32,128]{3,2,1,0:T(8,128)(2,1)} %param.5) | copy-start | bytes 786436
  38.8 16.4 %collective-permute-start.16 = (bf16[8,16,128]{2,1,0:T(8,128)(2,1)S(1)}, bf16[8,16,128]{2,1,0:T(8,128)(2,1)S(1)}, u32[]{:S(2)}, u32[]{:S(2)}) collective-permute-start(bf16[8,16,128]{2,1,0:T(8,128)(2,1)S(1)} %get-tuple-element.21), channel_id=1, source_target_pairs={{0,4},{4,8},{8,12},{12,16},{16,20},{20,24},{24,28},{1,5},{5,9},{9,... | collective-permute-start | bytes 98312 | tf_op jit(solution)/shard_map/ppermute | solution.py:14
  41.1 18.4 %collective-permute-start.17 = (bf16[8,16,128]{2,1,0:T(8,128)(2,1)S(1)}, bf16[8,16,128]{2,1,0:T(8,128)(2,1)S(1)}, u32[]{:S(2)}, u32[]{:S(2)}) collective-permute-start(bf16[8,16,128]{2,1,0:T(8,128)(2,1)S(1)} %get-tuple-element.22), channel_id=1, source_target_pairs={{4,0},{8,4},{12,8},{16,12},{20,16},{24,20},{28,24},{5,1},{9,5},{13... | collective-permute-start | bytes 98312 | tf_op jit(solution)/shard_map/ppermute | solution.py:15
  45.7 15.9 %collective-permute-start.4 = (bf16[8,16,128]{2,1,0:T(8,128)(2,1)S(1)}, bf16[8,16,128]{2,1,0:T(8,128)(2,1)S(1)}, u32[]{:S(2)}, u32[]{:S(2)}) collective-permute-start(bf16[8,16,128]{2,1,0:T(8,128)(2,1)S(1)} %get-tuple-element.15), channel_id=1, source_target_pairs={{0,4},{4,8},{8,12},{12,16},{16,20},{20,24},{24,28},{1,5},{5,9},{9,... | collective-permute-start | bytes 98312 | tf_op jit(solution)/shard_map/ppermute | solution.py:14
  47.7 18.0 %collective-permute-start.5 = (bf16[8,16,128]{2,1,0:T(8,128)(2,1)S(1)}, bf16[8,16,128]{2,1,0:T(8,128)(2,1)S(1)}, u32[]{:S(2)}, u32[]{:S(2)}) collective-permute-start(bf16[8,16,128]{2,1,0:T(8,128)(2,1)S(1)} %get-tuple-element.16), channel_id=1, source_target_pairs={{4,0},{8,4},{12,8},{16,12},{20,16},{24,20},{28,24},{5,1},{9,5},{13... | collective-permute-start | bytes 98312 | tf_op jit(solution)/shard_map/ppermute | solution.py:15
  52.9 17.0 %collective-permute-start.8 = (bf16[8,16,128]{2,1,0:T(8,128)(2,1)S(1)}, bf16[8,16,128]{2,1,0:T(8,128)(2,1)S(1)}, u32[]{:S(2)}, u32[]{:S(2)}) collective-permute-start(bf16[8,16,128]{2,1,0:T(8,128)(2,1)S(1)} %get-tuple-element.17), channel_id=1, source_target_pairs={{0,4},{4,8},{8,12},{12,16},{16,20},{20,24},{24,28},{1,5},{5,9},{9,... | collective-permute-start | bytes 98312 | tf_op jit(solution)/shard_map/ppermute | solution.py:14
  55.3 16.6 %collective-permute-start.9 = (bf16[8,16,128]{2,1,0:T(8,128)(2,1)S(1)}, bf16[8,16,128]{2,1,0:T(8,128)(2,1)S(1)}, u32[]{:S(2)}, u32[]{:S(2)}) collective-permute-start(bf16[8,16,128]{2,1,0:T(8,128)(2,1)S(1)} %get-tuple-element.18), channel_id=1, source_target_pairs={{4,0},{8,4},{12,8},{16,12},{20,16},{24,20},{28,24},{5,1},{9,5},{13... | collective-permute-start | bytes 98312 | tf_op jit(solution)/shard_map/ppermute | solution.py:15
  59.4 16.3 %collective-permute-start.12 = (bf16[8,16,128]{2,1,0:T(8,128)(2,1)S(1)}, bf16[8,16,128]{2,1,0:T(8,128)(2,1)S(1)}, u32[]{:S(2)}, u32[]{:S(2)}) collective-permute-start(bf16[8,16,128]{2,1,0:T(8,128)(2,1)S(1)} %get-tuple-element.19), channel_id=1, source_target_pairs={{0,4},{4,8},{8,12},{12,16},{16,20},{20,24},{24,28},{1,5},{5,9},{9,... | collective-permute-start | bytes 98312 | tf_op jit(solution)/shard_map/ppermute | solution.py:14
  61.6 16.0 %collective-permute-start.13 = (bf16[8,16,128]{2,1,0:T(8,128)(2,1)S(1)}, bf16[8,16,128]{2,1,0:T(8,128)(2,1)S(1)}, u32[]{:S(2)}, u32[]{:S(2)}) collective-permute-start(bf16[8,16,128]{2,1,0:T(8,128)(2,1)S(1)} %get-tuple-element.20), channel_id=1, source_target_pairs={{4,0},{8,4},{12,8},{16,12},{20,16},{24,20},{28,24},{5,1},{9,5},{13... | collective-permute-start | bytes 98312 | tf_op jit(solution)/shard_map/ppermute | solution.py:15
  65.8 25.1 %collective-permute-start.18 = (bf16[8,64,16]{2,1,0:T(8,128)(2,1)S(1)}, bf16[8,64,16]{2,1,0:T(8,128)(2,1)S(1)}, u32[]{:S(2)}, u32[]{:S(2)}) collective-permute-start(bf16[8,64,16]{2,1,0:T(8,128)(2,1)S(1)} %get-tuple-element.11), channel_id=1, source_target_pairs={{0,1},{1,2},{2,3},{4,5},{5,6},{6,7},{8,9},{9,10},{10,11},{12,13},{... | collective-permute-start | bytes 49160 | tf_op jit(solution)/shard_map/ppermute | solution.py:14
  69.9 21.0 %collective-permute-start.19 = (bf16[8,64,16]{2,1,0:T(8,128)(2,1)S(1)}, bf16[8,64,16]{2,1,0:T(8,128)(2,1)S(1)}, u32[]{:S(2)}, u32[]{:S(2)}) collective-permute-start(bf16[8,64,16]{2,1,0:T(8,128)(2,1)S(1)} %get-tuple-element.12), channel_id=1, source_target_pairs={{1,0},{2,1},{3,2},{5,4},{6,5},{7,6},{9,8},{10,9},{11,10},{13,12},{... | collective-permute-start | bytes 49160 | tf_op jit(solution)/shard_map/ppermute | solution.py:15
  71.9 19.8 %collective-permute-start.6 = (bf16[8,64,16]{2,1,0:T(8,128)(2,1)S(1)}, bf16[8,64,16]{2,1,0:T(8,128)(2,1)S(1)}, u32[]{:S(2)}, u32[]{:S(2)}) collective-permute-start(bf16[8,64,16]{2,1,0:T(8,128)(2,1)S(1)} %get-tuple-element.5), channel_id=1, source_target_pairs={{0,1},{1,2},{2,3},{4,5},{5,6},{6,7},{8,9},{9,10},{10,11},{12,13},{... | collective-permute-start | bytes 49160 | tf_op jit(solution)/shard_map/ppermute | solution.py:14
  75.7 4.5 %collective-permute-start.10 = (bf16[8,64,16]{2,1,0:T(8,128)(2,1)S(1)}, bf16[8,64,16]{2,1,0:T(8,128)(2,1)S(1)}, u32[]{:S(2)}, u32[]{:S(2)}) collective-permute-start(bf16[8,64,16]{2,1,0:T(8,128)(2,1)S(1)} %get-tuple-element.7), channel_id=1, source_target_pairs={{0,1},{1,2},{2,3},{4,5},{5,6},{6,7},{8,9},{9,10},{10,11},{12,13},{... | collective-permute-start | bytes 49160 | tf_op jit(solution)/shard_map/ppermute | solution.py:14
  77.6 6.3 %collective-permute-start.11 = (bf16[8,64,16]{2,1,0:T(8,128)(2,1)S(1)}, bf16[8,64,16]{2,1,0:T(8,128)(2,1)S(1)}, u32[]{:S(2)}, u32[]{:S(2)}) collective-permute-start(bf16[8,64,16]{2,1,0:T(8,128)(2,1)S(1)} %get-tuple-element.8), channel_id=1, source_target_pairs={{1,0},{2,1},{3,2},{5,4},{6,5},{7,6},{9,8},{10,9},{11,10},{13,12},{... | collective-permute-start | bytes 49160 | tf_op jit(solution)/shard_map/ppermute | solution.py:15
  80.2 6.4 %collective-permute-start.14 = (bf16[8,64,16]{2,1,0:T(8,128)(2,1)S(1)}, bf16[8,64,16]{2,1,0:T(8,128)(2,1)S(1)}, u32[]{:S(2)}, u32[]{:S(2)}) collective-permute-start(bf16[8,64,16]{2,1,0:T(8,128)(2,1)S(1)} %get-tuple-element.9), channel_id=1, source_target_pairs={{0,1},{1,2},{2,3},{4,5},{5,6},{6,7},{8,9},{9,10},{10,11},{12,13},{... | collective-permute-start | bytes 49160 | tf_op jit(solution)/shard_map/ppermute | solution.py:14
  83.9 6.3 %collective-permute-start.15 = (bf16[8,64,16]{2,1,0:T(8,128)(2,1)S(1)}, bf16[8,64,16]{2,1,0:T(8,128)(2,1)S(1)}, u32[]{:S(2)}, u32[]{:S(2)}) collective-permute-start(bf16[8,64,16]{2,1,0:T(8,128)(2,1)S(1)} %get-tuple-element.10), channel_id=1, source_target_pairs={{1,0},{2,1},{3,2},{5,4},{6,5},{7,6},{9,8},{10,9},{11,10},{13,12},{... | collective-permute-start | bytes 49160 | tf_op jit(solution)/shard_map/ppermute | solution.py:15
  86.6 6.3 %collective-permute-start.7 = (bf16[8,64,16]{2,1,0:T(8,128)(2,1)S(1)}, bf16[8,64,16]{2,1,0:T(8,128)(2,1)S(1)}, u32[]{:S(2)}, u32[]{:S(2)}) collective-permute-start(bf16[8,64,16]{2,1,0:T(8,128)(2,1)S(1)} %get-tuple-element.6), channel_id=1, source_target_pairs={{1,0},{2,1},{3,2},{5,4},{6,5},{7,6},{9,8},{10,9},{11,10},{13,12},{... | collective-permute-start | bytes 49160 | tf_op jit(solution)/shard_map/ppermute | solution.py:15
  91.6 1.6 %copy-start = (f32[8,32,128]{2,1,0:T(8,128)S(1)}, f32[8,32,128]{2,1,0:T(8,128)}, u32[]{:S(2)}) copy-start(f32[8,32,128]{2,1,0:T(8,128)} %param.4) | copy-start | bytes 393220
where the time goes:
time: 94.9 us; the launch traced here: 94.3 us
  starting transfers between devices  58.5 us (62%)
  matrix products  24.9 us (26%)
  waiting for transfers between devices  5.92 us (6%)
  other arithmetic  3.7 us (4%)
    ppermute x10, starting transfers between devices, extended_2(): after = lax.ppermute(leading, axis, down)  29.5 us
    ppermute x10, starting transfers between devices, extended_2(): before = lax.ppermute(last, axis, up)  29 us
    dot_general x16, matrix products, band_matrix(): jnp.einsum('ijt,t->ij', matches, kernel, precision=lax.Precision.HIGHEST)  18.9 us
    ppermute x10, waiting for transfers between devices, extended_2(): after = lax.ppermute(leading, axis, down)  5.9 us
    dot_general x8, matrix products, blur_block(): jnp.einsum('zyj,xj->zyx', padded, band_x, precision=lax.Precision.HIGHEST)  3.19 us
    dot_general x8, matrix products, blur_block(): jnp.einsum('zjx,yj->zyx', across, band_y, precision=lax.Precision.HIGHEST)  2.84 us
  transfers between devices with their start and end apart: 20, of which 3 were waited for; matrix products, arithmetic and copies ran while one was open for 27% of the time, Pallas kernels for 0%

commit v1 on v0

v1 whole, which is shorter than its diff:
```python
import functools

import jax
import jax.numpy as jnp
from jax import lax
from jax.experimental import pallas as pl
from jax.experimental.pallas import tpu as pltpu
from jax.sharding import PartitionSpec as P

BF = jnp.bfloat16
F32 = jnp.float32
MESH = pl.DeviceIdType.MESH


def dot(a, b, contract_b=0):
    return lax.dot_general(
        a, b, (((1,), (contract_b,)), ((), ())), preferred_element_type=F32
    )


def kernel(
    nr, nc, reach,
    est_hbm, views_hbm, pr_hbm, pc_hbm, out_ref,
    est_v, views_v, vu, vd, pr_v, pc_v, kp, ky_s, kt_s, df_s, da_s,
    ext, ybuf, recip, edge, edge_l, edge_r, gbuf, gedge, gedge_l, gedge_r,
    local_sem, send_sem, recv_sem,
):
    views, planes, height, width = views_v.shape
    taps = pr_v.shape[1]
    inner = height + 2 * reach
    outer = height + 4 * reach
    per = width // (2 * reach)
    groups = planes // per
    r, c = lax.axis_index("row"), lax.axis_index("col")
    up, down = (r - 1, c), (r + 1, c)
    left, right = (r, c - 1), (r, c + 1)
    has_up, has_down, has_left, has_right = r > 0, r < nr - 1, c > 0, c < nc - 1
    sides = ((has_up, up), (has_down, down), (has_left, left), (has_right, right))

    local = [
        pltpu.make_async_copy(s, d, local_sem.at[i])
        for i, (s, d) in enumerate(
            ((est_hbm, est_v), (pr_hbm, pr_v), (pc_hbm, pc_v), (views_hbm, views_v))
        )
    ]
    for copy in local:
        copy.start()

    barrier = pltpu.get_barrier_semaphore()
    for has, where in sides:
        @pl.when(has)
        def _():
            pl.semaphore_signal(barrier, inc=1, device_id=where, device_id_type=MESH)

    def remote(src, dst, slot, where):
        return pltpu.make_async_remote_copy(
            src_ref=src, dst_ref=dst, send_sem=send_sem.at[slot],
            recv_sem=recv_sem.at[slot], device_id=where, device_id_type=MESH,
        )

    to_up = [
        remote(ext.at[1], ext.at[2], 1, up),
        remote(views_hbm.at[:, :, pl.ds(0, reach), :], vd, 3, up),
    ]
    to_down = [
        remote(ext.at[1], ext.at[0], 0, down),
        remote(views_hbm.at[:, :, pl.ds(height - reach, reach), :], vu, 2, down),
    ]
    to_left = [remote(edge, edge_r, 5, left), remote(gedge, gedge_r, 7, left)]
    to_right = [remote(edge, edge_l, 4, right), remote(gedge, gedge_l, 6, right)]

    def start(which):
        for has, copies in which:
            @pl.when(has)
            def _(copies=copies):
                copies.start()

    def arrive(which):
        for has, copies in which:
            @pl.when(has)
            def _(copies=copies):
                copies.wait_recv()

    local[0].wait()
    for p in range(planes):
        ext[1, :, p * width:(p + 1) * width] = est_v[p].astype(BF)
    peers = 0
    for has, where in sides:
        peers = peers + has.astype(jnp.int32)
    pl.semaphore_wait(barrier, peers)
    start(((has_up, to_up[0]), (has_down, to_down[0])))
    start(((has_up, to_up[1]), (has_down, to_down[1])))

    for has, refs in (
        (has_up, (ext.at[0], vu)), (has_down, (ext.at[2], vd)),
        (has_left, (edge_l, gedge_l)), (has_right, (edge_r, gedge_r)),
    ):
        @pl.when(jnp.logical_not(has))
        def _(refs=refs):
            for ref in refs:
                ref[...] = jnp.zeros(ref.shape, ref.dtype)

    local[1].wait()
    local[2].wait()
    kp[...] = jnp.zeros(kp.shape, F32)
    psf_y, psf_x = pr_v[...], pc_v[...]
    kp[0:views, 0:taps] = psf_y / jnp.sum(psf_y, axis=1, keepdims=True)
    kp[views:2 * views, 0:taps] = psf_x / jnp.sum(psf_x, axis=1, keepdims=True)
    square = (width, width)
    apart = lax.broadcasted_iota(jnp.int32, square, 1) - lax.broadcasted_iota(jnp.int32, square, 0)
    near = (apart <= reach) & (apart >= -reach)
    for v in range(views):
        rows_y = jnp.broadcast_to(kp[v:v + 1, :], square)
        by = pltpu.roll(rows_y, 0, 1, stride=1, stride_axis=0)
        ky_s[v * inner:(v + 1) * inner, :] = by[:inner, :outer].astype(BF)
        kt_s[v] = by.T[2 * reach:2 * reach + height, :inner].astype(BF)
        rows_x = jnp.broadcast_to(kp[views + v:views + v + 1, :], square)
        bx = pltpu.roll(rows_x, width - reach, 1, stride=1, stride_axis=0)
        core = jnp.where(near, bx, 0.0).astype(BF)
        off = jnp.where(near, 0.0, bx).astype(BF)
        df_s[v, :, :width] = core
        df_s[v, :, width:] = off
        da_s[v, :width, :] = core
        da_s[v, width:, :] = off

    lane = lax.broadcasted_iota(jnp.int32, (8, width), 1)
    slot_of = ((lane + reach) // (2 * reach)) % per
    from_right = (lane // reach) % 2 == 0

    def mask(m, rows):
        return jnp.broadcast_to(m[:1], (rows, width))

    def pack(tiles):
        rows = tiles[0].shape[0]
        total = tiles[0]
        for k in range(1, per):
            total = jnp.where(mask(slot_of, rows) == k, pltpu.roll(tiles[k], 2 * reach * k, 1), total)
        return total

    arrive(((has_up, to_down[0]), (has_down, to_up[0])))
    e_all = ext[...].reshape(outer, planes * width)
    for g in range(groups):
        tiles = [
            e_all[:, (g * per + k) * width:(g * per + k + 1) * width].astype(F32)
            for k in range(per)
        ]
        edge[:, g * width:(g + 1) * width] = pack(tiles).astype(BF)
    start(((has_left, to_left[0]), (has_right, to_right[0])))
    ybuf[...] = dot(ky_s[...], e_all).astype(BF)
    arrive(((has_left, to_right[0]), (has_right, to_left[0])))
    sel = jnp.concatenate([mask(from_right, outer)] * groups, axis=1)
    edges = jnp.where(sel, edge_r[...].astype(F32), edge_l[...].astype(F32)).astype(BF)
    y_edges = dot(ky_s[...], edges)

    def unpack(tile, k):
        return tile if k == 0 else pltpu.roll(tile, width - 2 * reach * k, 1)

    row = lax.broadcasted_iota(jnp.int32, (inner, width), 0)
    inside = ((row >= reach) | has_up) & ((row < inner - reach) | has_down)
    for v in range(views):
        vs = slice(v * inner, (v + 1) * inner)
        parts = []
        for p in range(planes):
            g, k = divmod(p, per)
            halo = unpack(y_edges[vs, g * width:(g + 1) * width], k).astype(BF)
            parts.append(jnp.concatenate([ybuf[vs, p * width:(p + 1) * width], halo], axis=1))
        blurred = dot(jnp.concatenate(parts, axis=0), df_s[v], 1)
        for p in range(planes):
            b = blurred[p * inner:(p + 1) * inner]
            recip[v, p] = jnp.where(inside, 1.0 / b, 0.0)

    local[3].wait()
    arrive(((has_up, to_down[1]), (has_down, to_up[1])))
    for v in range(views):
        quot = []
        for p in range(planes):
            data = jnp.concatenate(
                [vu[v, p].astype(F32), views_v[v, p].astype(F32), vd[v, p].astype(F32)], axis=0
            )
            quot.append((data * recip[v, p]).astype(BF))
        g_v = dot(kt_s[v], jnp.concatenate(quot, axis=1))
        gbuf[v] = g_v
        for g in range(groups):
            tiles = [g_v[:, (g * per + k) * width:(g * per + k + 1) * width] for k in range(per)]
            gedge[v, :, g * width:(g + 1) * width] = pack(tiles).astype(BF)
    start(((has_left, to_left[1]), (has_right, to_right[1])))
    arrive(((has_left, to_right[1]), (has_right, to_left[1])))

    sel = jnp.concatenate([mask(from_right, height)] * groups, axis=1)
    product = None
    for v in range(views):
        halo = jnp.where(sel, gedge_r[v].astype(F32), gedge_l[v].astype(F32))
        parts, rest = [], []
        for p in range(planes):
            g, k = divmod(p, per)
            own = gbuf[v, :, p * width:(p + 1) * width]
            high = own.astype(BF)
            rest.append((own - high.astype(F32)).astype(BF))
            side = unpack(halo[:, g * width:(g + 1) * width], k).astype(BF)
            parts.append(jnp.concatenate([high, side], axis=1))
        corr = dot(jnp.concatenate(parts, axis=0), da_s[v])
        corr = corr + dot(jnp.concatenate(rest, axis=0), da_s[v, :width, :])
        product = corr if product is None else product * corr
    out_ref[...] = product.reshape(planes, height, width)

    for has, copies in ((has_up, to_up), (has_down, to_down), (has_left, to_left), (has_right, to_right)):
        @pl.when(has)
        def _(copies=copies):
            for copy in copies:
                copy.wait_send()


def local_step(nr, nc, estimate, views_data, psf_rows, psf_cols):
    views, planes, height, width = views_data.shape
    taps = psf_rows.shape[1]
    reach = (taps - 1) // 2
    inner, outer = height + 2 * reach, height + 4 * reach
    per = width // (2 * reach)
    groups = planes // per
    vm = pltpu.VMEM
    any_spec = pl.BlockSpec(memory_space=pl.ANY)
    product = pl.pallas_call(
        functools.partial(kernel, nr, nc, reach),
        out_shape=jax.ShapeDtypeStruct((planes, height, width), F32),
        in_specs=[any_spec] * 4,
        out_specs=pl.BlockSpec(memory_space=pltpu.VMEM),
        scratch_shapes=[
            vm((planes, height, width), F32),
            vm((views, planes, height, width), BF),
            vm((views, planes, reach, width), BF),
            vm((views, planes, reach, width), BF),
            vm((views, taps), F32),
            vm((views, taps), F32),
            vm((2 * views, width), F32),
            vm((views * inner, outer), BF),
            vm((views, height, inner), BF),
            vm((views, width, 2 * width), BF),
            vm((views, 2 * width, width), BF),
            vm((3, height, planes * width), BF),
            vm((views * inner, planes * width), BF),
            vm((views, planes, inner, width), F32),
            vm((outer, groups * width), BF),
            vm((outer, groups * width), BF),
            vm((outer, groups * width), BF),
            vm((views, height, planes * width), F32),
            vm((views, height, groups * width), BF),
            vm((views, height, groups * width), BF),
            vm((views, height, groups * width), BF),
            pltpu.SemaphoreType.DMA((4,)),
            pltpu.SemaphoreType.DMA((8,)),
            pltpu.SemaphoreType.DMA((8,)),
        ],
        compiler_params=pltpu.CompilerParams(
            collective_id=0, has_side_effects=True, vmem_limit_bytes=32 * 1024 * 1024
        ),
        name="deconvolve",
    )(estimate, views_data, psf_rows, psf_cols)
    return estimate * jnp.sqrt(jnp.sqrt(product))


def solution(mesh):
    nr, nc = mesh.shape["row"], mesh.shape["col"]
    return jax.shard_map(
        functools.partial(local_step, nr, nc),
        mesh=mesh,
        in_specs=(P(None, "row", "col"), P(None, None, "row", "col"), P(), P()),
        out_specs=P(None, "row", "col"),
        check_vma=False,
    )
```

time: 94.9 us -> 21.2 us (0.22)
  starting transfers between devices: 58.5 us -> 0 us
  matrix products: 24.9 us -> 0 us
  Pallas kernels: 0 us -> 17 us
  waiting for transfers between devices: 5.92 us -> 0 us
  other arithmetic: 3.7 us -> 0.73 us
  local copies, waits for them, and re-layouts: 0.61 us -> 3.22 us
    ppermute x20 -> x0, starting transfers between devices: 58.5 us -> none  [the longest x10 29.5 us: extended_2(): after = lax.ppermute(leading, axis, down)]
    dot_general x32 -> x0, matrix products: 24.9 us -> none  [the longest x16 18.9 us: band_matrix(): jnp.einsum('ijt,t->ij', matches, kernel, precision=lax.Precision.HIGHEST)]
    pallas_call x0 -> x1, Pallas kernels: none -> 17 us  [local_step(): pl.pallas_call(functools.partial(kernel, nr, nc, reach), out_shape=jax.Sh...]
    ppermute x20 -> x0, waiting for transfers between devices: 5.92 us -> none  [the longest x10 5.9 us: extended_2(): after = lax.ppermute(leading, axis, down)]
    unnamed x6 -> x8, local copies, waits for them, and re-layouts: 0.01 us -> 3.22 us
  transfers between devices with their start and end apart: 20 -> 0, of which waited for: 3 -> 0; matrix products, arithmetic and copies ran while one was open for 27% -> 0% of each run, Pallas kernels for 0% -> 0%
where the time goes in v1:
time: 21.2 us; the launch traced here: 20.9 us
  Pallas kernels  17 us (80%)
  local copies, waits for them, and re-layouts  3.22 us (15%)
  other arithmetic  0.73 us (3%)
    pallas_call x1, Pallas kernels, local_step(): pl.pallas_call(functools.partial(kernel, nr, nc, reach), out_shape=jax.Sh...  17 us
    unnamed x8, local copies, waits for them, and re-layouts  3.22 us
    mul x1, other arithmetic, local_step(): return estimate * jnp.sqrt(jnp.sqrt(product))  0.73 us

profile of v1, /device:TPU:9, one launch (start us, length us, event | category | flops | bytes accessed | tf_op | source)
XLA Modules:
  0.0 20.9 jit_solution(17980498571373163665)
XLA Ops:
  0.0 0.0 copy-start
  0.0 0.9 %copy-done = f32[8,32,128]{2,1,0:T(8,128)S(1)} copy-done((f32[8,32,128]{2,1,0:T(8,128)S(1)}, f32[8,32,128]{2,1,0:T(8,128)}, u32[]{:S(2)}) %copy-start) | copy-done | bytes 131096
  0.9 0.0 copy-start.1
  0.9 0.9 %copy-done.1 = bf16[4,8,32,128]{3,2,1,0:T(8,128)(2,1)S(1)} copy-done((bf16[4,8,32,128]{3,2,1,0:T(8,128)(2,1)S(1)}, bf16[4,8,32,128]{3,2,1,0:T(8,128)(2,1)}, u32[]{:S(2)}) %copy-start.1) | copy-done | bytes 262168
  1.9 0.0 copy-start.2
  1.9 0.7 %copy-done.2 = f32[4,33]{1,0:T(4,128)S(1)} copy-done((f32[4,33]{1,0:T(4,128)S(1)}, f32[4,33]{1,0:T(4,128)}, u32[]{:S(2)}) %copy-start.2) | copy-done | bytes 552
  2.5 0.0 copy-start.3
  2.5 0.7 %copy-done.3 = f32[4,33]{1,0:T(4,128)S(1)} copy-done((f32[4,33]{1,0:T(4,128)S(1)}, f32[4,33]{1,0:T(4,128)}, u32[]{:S(2)}) %copy-start.3) | copy-done | bytes 552
  3.2 17.0 %deconvolve.1 = f32[8,32,128]{2,1,0:T(8,128)S(1)} custom-call(f32[8,32,128]{2,1,0:T(8,128)S(1)} %copy-done, bf16[4,8,32,128]{3,2,1,0:T(8,128)(2,1)S(1)} %copy-done.1, f32[4,33]{1,0:T(4,128)S(1)} %copy-done.2, f32[4,33]{1,0:T(4,128)S(1)} %copy-done.3), custom_call_target="tpu_custom_call" | custom-call | tf_op jit(solution)/shard_map/deconvolve/pallas_call | solution.py:222
  20.2 0.7 %sqrt_multiply_fusion = f32[8,32,128]{2,1,0:T(8,128)} fusion(f32[8,32,128]{2,1,0:T(8,128)S(1)} %copy-done, f32[8,32,128]{2,1,0:T(8,128)S(1)} %deconvolve.1), kind=kLoop, calls=%fused_computation | loop fusion | flops 32768 | bytes 393216 | tf_op jit(solution)/shard_map/mul | solution.py:258
Async XLA Ops:
  0.0 0.9 %copy-start = (f32[8,32,128]{2,1,0:T(8,128)S(1)}, f32[8,32,128]{2,1,0:T(8,128)}, u32[]{:S(2)}) copy-start(f32[8,32,128]{2,1,0:T(8,128)} %est_hbm.1) | copy-start | bytes 393220
  0.9 0.9 %copy-start.1 = (bf16[4,8,32,128]{3,2,1,0:T(8,128)(2,1)S(1)}, bf16[4,8,32,128]{3,2,1,0:T(8,128)(2,1)}, u32[]{:S(2)}) copy-start(bf16[4,8,32,128]{3,2,1,0:T(8,128)(2,1)} %views_hbm.1) | copy-start | bytes 786436
  1.9 0.7 %copy-start.2 = (f32[4,33]{1,0:T(4,128)S(1)}, f32[4,33]{1,0:T(4,128)}, u32[]{:S(2)}) copy-start(f32[4,33]{1,0:T(4,128)} %pr_hbm.1) | copy-start | bytes 1588
  2.5 0.7 %copy-start.3 = (f32[4,33]{1,0:T(4,128)S(1)}, f32[4,33]{1,0:T(4,128)}, u32[]{:S(2)}) copy-start(f32[4,33]{1,0:T(4,128)} %pc_hbm.1) | copy-start | bytes 1588

commit v2 on v1

--- a/solution.py
+++ b/solution.py
@@ -58,16 +58,25 @@
             recv_sem=recv_sem.at[slot], device_id=where, device_id_type=MESH,
         )
 
+    views_at, gedge_at = 4, 4 + 2 * views
     to_up = [
         remote(ext.at[1], ext.at[2], 1, up),
-        remote(views_hbm.at[:, :, pl.ds(0, reach), :], vd, 3, up),
+    ] + [
+        remote(views_hbm.at[v, :, pl.ds(0, reach), :], vd.at[v], views_at + views + v, up)
+        for v in range(views)
     ]
     to_down = [
         remote(ext.at[1], ext.at[0], 0, down),
-        remote(views_hbm.at[:, :, pl.ds(height - reach, reach), :], vu, 2, down),
-    ]
-    to_left = [remote(edge, edge_r, 5, left), remote(gedge, gedge_r, 7, left)]
-    to_right = [remote(edge, edge_l, 4, right), remote(gedge, gedge_l, 6, right)]
+    ] + [
+        remote(views_hbm.at[v, :, pl.ds(height - reach, reach), :], vu.at[v], views_at + v, down)
+        for v in range(views)
+    ]
+    to_left = [remote(edge, edge_r, 3, left)] + [
+        remote(gedge.at[v], gedge_r.at[v], gedge_at + views + v, left) for v in range(views)
+    ]
+    to_right = [remote(edge, edge_l, 2, right)] + [
+        remote(gedge.at[v], gedge_l.at[v], gedge_at + v, right) for v in range(views)
+    ]
 
     def start(which):
         for has, copies in which:
@@ -89,7 +98,8 @@
         peers = peers + has.astype(jnp.int32)
     pl.semaphore_wait(barrier, peers)
     start(((has_up, to_up[0]), (has_down, to_down[0])))
-    start(((has_up, to_up[1]), (has_down, to_down[1])))
+    for v in range(views):
+        start(((has_up, to_up[1 + v]), (has_down, to_down[1 + v])))
 
     for has, refs in (
         (has_up, (ext.at[0], vu)), (has_down, (ext.at[2], vd)),
@@ -169,9 +179,10 @@
             b = blurred[p * inner:(p + 1) * inner]
             recip[v, p] = jnp.where(inside, 1.0 / b, 0.0)
 
-    local[3].wait()
-    arrive(((has_up, to_down[1]), (has_down, to_up[1])))
-    for v in range(views):
+    sel = jnp.concatenate([mask(from_right, height)] * groups, axis=1)
+
+    def send_edges(v):
+        arrive(((has_up, to_down[1 + v]), (has_down, to_up[1 + v])))
         quot = []
         for p in range(planes):
             data = jnp.concatenate(
@@ -183,12 +194,10 @@
         for g in range(groups):
             tiles = [g_v[:, (g * per + k) * width:(g * per + k + 1) * width] for k in range(per)]
             gedge[v, :, g * width:(g + 1) * width] = pack(tiles).astype(BF)
-    start(((has_left, to_left[1]), (has_right, to_right[1])))
-    arrive(((has_left, to_right[1]), (has_right, to_left[1])))
-
-    sel = jnp.concatenate([mask(from_right, height)] * groups, axis=1)
-    product = None
-    for v in range(views):
+        start(((has_left, to_left[1 + v]), (has_right, to_right[1 + v])))
+
+    def corrected(v):
+        arrive(((has_left, to_right[1 + v]), (has_right, to_left[1 + v])))
         halo = jnp.where(sel, gedge_r[v].astype(F32), gedge_l[v].astype(F32))
         parts, rest = [], []
         for p in range(planes):
@@ -200,8 +209,15 @@
             parts.append(jnp.concatenate([high, side], axis=1))
         corr = dot(jnp.concatenate(parts, axis=0), da_s[v])
         corr = corr + dot(jnp.concatenate(rest, axis=0), da_s[v, :width, :])
-        product = corr if product is None else product * corr
-    out_ref[...] = product.reshape(planes, height, width)
+        corr = corr.reshape(planes, height, width)
+        out_ref[...] = corr if v == 0 else out_ref[...] * corr
+
+    local[3].wait()
+    for v in range(views):
+        send_edges(v)
+        if v > 0:
+            corrected(v - 1)
+    corrected(views - 1)
 
     for has, copies in ((has_up, to_up), (has_down, to_down), (has_left, to_left), (has_right, to_right)):
         @pl.when(has)
@@ -218,7 +234,7 @@
     per = width // (2 * reach)
     groups = planes // per
     vm = pltpu.VMEM
-    any_spec = pl.BlockSpec(memory_space=pl.ANY)
+    any_spec = pl.BlockSpec(memory_space=pltpu.HBM)
     product = pl.pallas_call(
         functools.partial(kernel, nr, nc, reach),
         out_shape=jax.ShapeDtypeStruct((planes, height, width), F32),
@@ -247,11 +263,11 @@
             vm((views, height, groups * width), BF),
             vm((views, height, groups * width), BF),
             pltpu.SemaphoreType.DMA((4,)),
-            pltpu.SemaphoreType.DMA((8,)),
-            pltpu.SemaphoreType.DMA((8,)),
+            pltpu.SemaphoreType.DMA((4 + 4 * views,)),
+            pltpu.SemaphoreType.DMA((4 + 4 * views,)),
         ],
         compiler_params=pltpu.CompilerParams(
-            collective_id=0, has_side_effects=True, vmem_limit_bytes=32 * 1024 * 1024
+            collective_id=0, has_side_effects=True, vmem_limit_bytes=48 * 1024 * 1024
         ),
         name="deconvolve",
     )(estimate, views_data, psf_rows, psf_cols)

time: 21.2 us -> 24.2 us (1.14)
  Pallas kernels: 17 us -> 20 us
    pallas_call x1, Pallas kernels: 17 us -> 20 us  [local_step(): pl.pallas_call(functools.partial(kernel, nr, nc, reach), out_shape=jax.Sh...]
where the time goes in v2:
time: 24.2 us; the launch traced here: 23.9 us
  Pallas kernels  20 us (83%)
  local copies, waits for them, and re-layouts  3.22 us (13%)
  other arithmetic  0.73 us (3%)
    pallas_call x1, Pallas kernels, local_step(): pl.pallas_call(functools.partial(kernel, nr, nc, reach), out_shape=jax.Sh...  20 us
    unnamed x8, local copies, waits for them, and re-layouts  3.22 us
    mul x1, other arithmetic, local_step(): return estimate * jnp.sqrt(jnp.sqrt(product))  0.73 us

profile of v2, /device:TPU:9, one launch (start us, length us, event | category | flops | bytes accessed | tf_op | source)
XLA Modules:
  0.0 23.9 jit_solution(17099311382178360259)
XLA Ops:
  0.0 0.0 copy-start
  0.0 0.9 %copy-done = f32[8,32,128]{2,1,0:T(8,128)S(1)} copy-done((f32[8,32,128]{2,1,0:T(8,128)S(1)}, f32[8,32,128]{2,1,0:T(8,128)}, u32[]{:S(2)}) %copy-start) | copy-done | bytes 131096
  0.9 0.0 copy-start.1
  0.9 0.9 %copy-done.1 = bf16[4,8,32,128]{3,2,1,0:T(8,128)(2,1)S(1)} copy-done((bf16[4,8,32,128]{3,2,1,0:T(8,128)(2,1)S(1)}, bf16[4,8,32,128]{3,2,1,0:T(8,128)(2,1)}, u32[]{:S(2)}) %copy-start.1) | copy-done | bytes 262168
  1.9 0.0 copy-start.2
  1.9 0.7 %copy-done.2 = f32[4,33]{1,0:T(4,128)S(1)} copy-done((f32[4,33]{1,0:T(4,128)S(1)}, f32[4,33]{1,0:T(4,128)}, u32[]{:S(2)}) %copy-start.2) | copy-done | bytes 552
  2.5 0.0 copy-start.3
  2.5 0.7 %copy-done.3 = f32[4,33]{1,0:T(4,128)S(1)} copy-done((f32[4,33]{1,0:T(4,128)S(1)}, f32[4,33]{1,0:T(4,128)}, u32[]{:S(2)}) %copy-start.3) | copy-done | bytes 552
  3.2 20.0 %deconvolve.1 = f32[8,32,128]{2,1,0:T(8,128)S(1)} custom-call(f32[8,32,128]{2,1,0:T(8,128)S(1)} %copy-done, bf16[4,8,32,128]{3,2,1,0:T(8,128)(2,1)S(1)} %copy-done.1, f32[4,33]{1,0:T(4,128)S(1)} %copy-done.2, f32[4,33]{1,0:T(4,128)S(1)} %copy-done.3), custom_call_target="tpu_custom_call" | custom-call | tf_op jit(solution)/shard_map/deconvolve/pallas_call | solution.py:238
  23.2 0.7 %sqrt_multiply_fusion = f32[8,32,128]{2,1,0:T(8,128)} fusion(f32[8,32,128]{2,1,0:T(8,128)S(1)} %copy-done, f32[8,32,128]{2,1,0:T(8,128)S(1)} %deconvolve.1), kind=kLoop, calls=%fused_computation | loop fusion | flops 32768 | bytes 393216 | tf_op jit(solution)/shard_map/mul | solution.py:274
Async XLA Ops:
  0.0 0.9 %copy-start = (f32[8,32,128]{2,1,0:T(8,128)S(1)}, f32[8,32,128]{2,1,0:T(8,128)}, u32[]{:S(2)}) copy-start(f32[8,32,128]{2,1,0:T(8,128)} %est_hbm.1) | copy-start | bytes 393220
  0.9 0.9 %copy-start.1 = (bf16[4,8,32,128]{3,2,1,0:T(8,128)(2,1)S(1)}, bf16[4,8,32,128]{3,2,1,0:T(8,128)(2,1)}, u32[]{:S(2)}) copy-start(bf16[4,8,32,128]{3,2,1,0:T(8,128)(2,1)} %views_hbm.1) | copy-start | bytes 786436
  1.9 0.7 %copy-start.2 = (f32[4,33]{1,0:T(4,128)S(1)}, f32[4,33]{1,0:T(4,128)}, u32[]{:S(2)}) copy-start(f32[4,33]{1,0:T(4,128)} %pr_hbm.1) | copy-start | bytes 1588
  2.5 0.7 %copy-start.3 = (f32[4,33]{1,0:T(4,128)S(1)}, f32[4,33]{1,0:T(4,128)}, u32[]{:S(2)}) copy-start(f32[4,33]{1,0:T(4,128)} %pc_hbm.1) | copy-start | bytes 1588

commit v3 on v2

--- a/solution.py
+++ b/solution.py
@@ -62,13 +62,13 @@
     to_up = [
         remote(ext.at[1], ext.at[2], 1, up),
     ] + [
-        remote(views_hbm.at[v, :, pl.ds(0, reach), :], vd.at[v], views_at + views + v, up)
+        remote(views_v.at[v, :, pl.ds(0, reach), :], vd.at[v], views_at + views + v, up)
         for v in range(views)
     ]
     to_down = [
         remote(ext.at[1], ext.at[0], 0, down),
     ] + [
-        remote(views_hbm.at[v, :, pl.ds(height - reach, reach), :], vu.at[v], views_at + v, down)
+        remote(views_v.at[v, :, pl.ds(height - reach, reach), :], vu.at[v], views_at + v, down)
         for v in range(views)
     ]
     to_left = [remote(edge, edge_r, 3, left)] + [
@@ -98,6 +98,7 @@
         peers = peers + has.astype(jnp.int32)
     pl.semaphore_wait(barrier, peers)
     start(((has_up, to_up[0]), (has_down, to_down[0])))
+    local[3].wait()
     for v in range(views):
         start(((has_up, to_up[1 + v]), (has_down, to_down[1 + v])))
 
@@ -212,12 +213,10 @@
         corr = corr.reshape(planes, height, width)
         out_ref[...] = corr if v == 0 else out_ref[...] * corr
 
-    local[3].wait()
     for v in range(views):
         send_edges(v)
-        if v > 0:
-            corrected(v - 1)
-    corrected(views - 1)
+    for v in range(views):
+        corrected(v)
 
     for has, copies in ((has_up, to_up), (has_down, to_down), (has_left, to_left), (has_right, to_right)):
         @pl.when(has)
@@ -234,7 +233,7 @@
     per = width // (2 * reach)
     groups = planes // per
     vm = pltpu.VMEM
-    any_spec = pl.BlockSpec(memory_space=pltpu.HBM)
+    any_spec = pl.BlockSpec(memory_space=pl.ANY)
     product = pl.pallas_call(
         functools.partial(kernel, nr, nc, reach),
         out_shape=jax.ShapeDtypeStruct((planes, height, width), F32),
@@ -266,9 +265,7 @@
             pltpu.SemaphoreType.DMA((4 + 4 * views,)),
             pltpu.SemaphoreType.DMA((4 + 4 * views,)),
         ],
-        compiler_params=pltpu.CompilerParams(
-            collective_id=0, has_side_effects=True, vmem_limit_bytes=48 * 1024 * 1024
-        ),
+        compiler_params=pltpu.CompilerParams(collective_id=0, has_side_effects=True),
         name="deconvolve",
     )(estimate, views_data, psf_rows, psf_cols)
     return estimate * jnp.sqrt(jnp.sqrt(product))

time: 24.2 us -> 19.5 us (0.81)
  local copies, waits for them, and re-layouts: 3.22 us -> 0.01 us
  Pallas kernels: 20 us -> 17.7 us
  other arithmetic: 0.73 us -> 1.63 us
    unnamed x8 -> x2, local copies, waits for them, and re-layouts: 3.22 us -> 0.01 us
    pallas_call x1, Pallas kernels: 20 us -> 17.7 us  [local_step(): pl.pallas_call(functools.partial(kernel, nr, nc, reach), out_shape=jax.Sh...]
    mul x1, other arithmetic: 0.73 us -> 1.63 us  [local_step(): return estimate * jnp.sqrt(jnp.sqrt(product))]
where the time goes in v3:
time: 19.5 us; the launch traced here: 19.3 us
  Pallas kernels  17.7 us (91%)
  other arithmetic  1.63 us (8%)
    pallas_call x1, Pallas kernels, local_step(): pl.pallas_call(functools.partial(kernel, nr, nc, reach), out_shape=jax.Sh...  17.7 us
    mul x1, other arithmetic, local_step(): return estimate * jnp.sqrt(jnp.sqrt(product))  1.63 us

profile of v3, /device:TPU:9, one launch (start us, length us, event | category | flops | bytes accessed | tf_op | source)
XLA Modules:
  0.0 19.3 jit_solution(9827836770136330719)
XLA Ops:
  0.0 0.0 copy-start
  0.0 17.7 %deconvolve.1 = f32[8,32,128]{2,1,0:T(8,128)} custom-call(f32[8,32,128]{2,1,0:T(8,128)} %est_hbm.1, bf16[4,8,32,128]{3,2,1,0:T(8,128)(2,1)} %views_hbm.1, f32[4,33]{1,0:T(4,128)} %pr_hbm.1, f32[4,33]{1,0:T(4,128)} %pc_hbm.1), custom_call_target="tpu_custom_call" | custom-call | tf_op jit(solution)/shard_map/deconvolve/pallas_call | solution.py:237
  17.7 0.0 copy-done
  17.7 1.6 %sqrt_multiply_fusion = f32[8,32,128]{2,1,0:T(8,128)} fusion(f32[8,32,128]{2,1,0:T(8,128)S(1)} %copy-done, f32[8,32,128]{2,1,0:T(8,128)} %deconvolve.1), kind=kLoop, calls=%fused_computation | loop fusion | flops 32768 | bytes 393216 | tf_op jit(solution)/shard_map/mul | solution.py:271
Async XLA Ops:
  0.0 17.7 %copy-start = (f32[8,32,128]{2,1,0:T(8,128)S(1)}, f32[8,32,128]{2,1,0:T(8,128)}, u32[]{:S(2)}) copy-start(f32[8,32,128]{2,1,0:T(8,128)} %est_hbm.1) | copy-start | bytes 393220

commit v4 on v3

--- a/solution.py
+++ b/solution.py
@@ -98,10 +98,6 @@
         peers = peers + has.astype(jnp.int32)
     pl.semaphore_wait(barrier, peers)
     start(((has_up, to_up[0]), (has_down, to_down[0])))
-    local[3].wait()
-    for v in range(views):
-        start(((has_up, to_up[1 + v]), (has_down, to_down[1 + v])))
-
     for has, refs in (
         (has_up, (ext.at[0], vu)), (has_down, (ext.at[2], vd)),
         (has_left, (edge_l, gedge_l)), (has_right, (edge_r, gedge_r)),
@@ -147,6 +143,14 @@
         for k in range(1, per):
             total = jnp.where(mask(slot_of, rows) == k, pltpu.roll(tiles[k], 2 * reach * k, 1), total)
         return total
+
+    local[3].wait()
+    for has, copies in ((has_up, to_up), (has_down, to_down)):
+        @pl.when(has)
+        def _(copies=copies):
+            copies[0].wait_send()
+    for v in range(views):
+        start(((has_up, to_up[1 + v]), (has_down, to_down[1 + v])))
 
     arrive(((has_up, to_down[0]), (has_down, to_up[0])))
     e_all = ext[...].reshape(outer, planes * width)
@@ -214,11 +218,15 @@
         out_ref[...] = corr if v == 0 else out_ref[...] * corr
 
     for v in range(views):
+        if v == views - 1:
+            corrected(0)
         send_edges(v)
-    for v in range(views):
+    for v in range(1, views):
         corrected(v)
 
-    for has, copies in ((has_up, to_up), (has_down, to_down), (has_left, to_left), (has_right, to_right)):
+    for has, copies in (
+        (has_up, to_up[1:]), (has_down, to_down[1:]), (has_left, to_left), (has_right, to_right)
+    ):
         @pl.when(has)
         def _(copies=copies):
             for copy in copies:

time: 19.5 us -> 22.1 us (1.13)
  Pallas kernels: 17.7 us -> 20.3 us
    pallas_call x1, Pallas kernels: 17.7 us -> 20.3 us  [local_step(): pl.pallas_call(functools.partial(kernel, nr, nc, reach), out_shape=jax.Sh...]
where the time goes in v4:
time: 22.1 us; the launch traced here: 22 us
  Pallas kernels  20.3 us (92%)
  other arithmetic  1.63 us (7%)
    pallas_call x1, Pallas kernels, local_step(): pl.pallas_call(functools.partial(kernel, nr, nc, reach), out_shape=jax.Sh...  20.3 us
    mul x1, other arithmetic, local_step(): return estimate * jnp.sqrt(jnp.sqrt(product))  1.63 us

profile of v4, /device:TPU:9, one launch (start us, length us, event | category | flops | bytes accessed | tf_op | source)
XLA Modules:
  0.0 22.0 jit_solution(14974789741537544163)
XLA Ops:
  0.0 0.0 copy-start
  0.0 20.3 %deconvolve.1 = f32[8,32,128]{2,1,0:T(8,128)} custom-call(f32[8,32,128]{2,1,0:T(8,128)} %est_hbm.1, bf16[4,8,32,128]{3,2,1,0:T(8,128)(2,1)} %views_hbm.1, f32[4,33]{1,0:T(4,128)} %pr_hbm.1, f32[4,33]{1,0:T(4,128)} %pc_hbm.1), custom_call_target="tpu_custom_call" | custom-call | tf_op jit(solution)/shard_map/deconvolve/pallas_call | solution.py:245
  20.3 0.0 copy-done
  20.3 1.6 %sqrt_multiply_fusion = f32[8,32,128]{2,1,0:T(8,128)} fusion(f32[8,32,128]{2,1,0:T(8,128)S(1)} %copy-done, f32[8,32,128]{2,1,0:T(8,128)} %deconvolve.1), kind=kLoop, calls=%fused_computation | loop fusion | flops 32768 | bytes 393216 | tf_op jit(solution)/shard_map/mul | solution.py:279
Async XLA Ops:
  0.0 20.3 %copy-start = (f32[8,32,128]{2,1,0:T(8,128)S(1)}, f32[8,32,128]{2,1,0:T(8,128)}, u32[]{:S(2)}) copy-start(f32[8,32,128]{2,1,0:T(8,128)} %est_hbm.1) | copy-start | bytes 393220

commit v5 on v3

--- a/solution.py
+++ b/solution.py
@@ -99,9 +99,7 @@
     pl.semaphore_wait(barrier, peers)
     start(((has_up, to_up[0]), (has_down, to_down[0])))
     local[3].wait()
-    for v in range(views):
-        start(((has_up, to_up[1 + v]), (has_down, to_down[1 + v])))
-
+    start(((has_up, to_up[1]), (has_down, to_down[1])))
     for has, refs in (
         (has_up, (ext.at[0], vu)), (has_down, (ext.at[2], vd)),
         (has_left, (edge_l, gedge_l)), (has_right, (edge_r, gedge_r)),
@@ -157,6 +155,8 @@
         ]
         edge[:, g * width:(g + 1) * width] = pack(tiles).astype(BF)
     start(((has_left, to_left[0]), (has_right, to_right[0])))
+    for v in range(1, views):
+        start(((has_up, to_up[1 + v]), (has_down, to_down[1 + v])))
     ybuf[...] = dot(ky_s[...], e_all).astype(BF)
     arrive(((has_left, to_right[0]), (has_right, to_left[0])))
     sel = jnp.concatenate([mask(from_right, outer)] * groups, axis=1)

time: 19.5 us -> 20.2 us (1.036)
  the two profiles are of different devices: /device:TPU:9 before, /device:TPU:11 now
where the time goes in v5:
time: 20.2 us; the launch traced here: 20 us
  Pallas kernels  18.4 us (91%)
  other arithmetic  1.63 us (8%)
    pallas_call x1, Pallas kernels, local_step(): pl.pallas_call(functools.partial(kernel, nr, nc, reach), out_shape=jax.Sh...  18.4 us
    mul x1, other arithmetic, local_step(): return estimate * jnp.sqrt(jnp.sqrt(product))  1.63 us

profile of v5, /device:TPU:11, one launch (start us, length us, event | category | flops | bytes accessed | tf_op | source)
XLA Modules:
  0.0 20.0 jit_solution(8499017538410895006)
XLA Ops:
  0.0 0.0 copy-start
  0.0 18.4 %deconvolve.1 = f32[8,32,128]{2,1,0:T(8,128)} custom-call(f32[8,32,128]{2,1,0:T(8,128)} %est_hbm.1, bf16[4,8,32,128]{3,2,1,0:T(8,128)(2,1)} %views_hbm.1, f32[4,33]{1,0:T(4,128)} %pr_hbm.1, f32[4,33]{1,0:T(4,128)} %pc_hbm.1), custom_call_target="tpu_custom_call" | custom-call | tf_op jit(solution)/shard_map/deconvolve/pallas_call | solution.py:237
  18.4 0.0 copy-done
  18.4 1.6 %sqrt_multiply_fusion = f32[8,32,128]{2,1,0:T(8,128)} fusion(f32[8,32,128]{2,1,0:T(8,128)S(1)} %copy-done, f32[8,32,128]{2,1,0:T(8,128)} %deconvolve.1), kind=kLoop, calls=%fused_computation | loop fusion | flops 32768 | bytes 393216 | tf_op jit(solution)/shard_map/mul | solution.py:271
Async XLA Ops:
  0.0 18.4 %copy-start = (f32[8,32,128]{2,1,0:T(8,128)S(1)}, f32[8,32,128]{2,1,0:T(8,128)}, u32[]{:S(2)}) copy-start(f32[8,32,128]{2,1,0:T(8,128)} %est_hbm.1) | copy-start | bytes 393220

commit v6 on v1

v6 whole, which is shorter than its diff:
```python
import functools

import jax
import jax.numpy as jnp
from jax import lax
from jax.experimental import pallas as pl
from jax.experimental.pallas import tpu as pltpu
from jax.sharding import PartitionSpec as P

BF = jnp.bfloat16
F32 = jnp.float32
MESH = pl.DeviceIdType.MESH


def dot(a, b, contract_b=0):
    return lax.dot_general(
        a, b, (((1,), (contract_b,)), ((), ())), preferred_element_type=F32
    )


def kernel(
    nr, nc, reach,
    est_hbm, views_hbm, pr_hbm, pc_hbm, out_ref,
    est_v, views_v, pr_v, pc_v, kp, ky_s, kt_s, df_s, da_s,
    ext, ybuf, quot, edge, edge_l, edge_r, gbuf, gedge, gedge_l, gedge_r,
    local_sem, send_sem, recv_sem,
):
    views, planes, height, width = views_v.shape
    taps = pr_v.shape[1]
    inner = height + 2 * reach
    per = width // (2 * reach)
    groups = planes // per
    r, c = lax.axis_index("row"), lax.axis_index("col")
    up, down = (r - 1, c), (r + 1, c)
    left, right = (r, c - 1), (r, c + 1)
    has_up, has_down, has_left, has_right = r > 0, r < nr - 1, c > 0, c < nc - 1
    corners = (
        (has_up & has_left, (r - 1, c - 1)), (has_up & has_right, (r - 1, c + 1)),
        (has_down & has_left, (r + 1, c - 1)), (has_down & has_right, (r + 1, c + 1)),
    )
    sides = ((has_up, up), (has_down, down), (has_left, left), (has_right, right)) + corners

    local = [
        pltpu.make_async_copy(s, d, local_sem.at[i])
        for i, (s, d) in enumerate(
            ((est_hbm, est_v), (pr_hbm, pr_v), (pc_hbm, pc_v), (views_hbm, views_v))
        )
    ]
    for copy in local:
        copy.start()

    barrier = pltpu.get_barrier_semaphore()
    for has, where in sides:
        @pl.when(has)
        def _():
            pl.semaphore_signal(barrier, inc=1, device_id=where, device_id_type=MESH)

    def remote(src, dst, slot, where):
        return pltpu.make_async_remote_copy(
            src_ref=src, dst_ref=dst, send_sem=send_sem.at[slot],
            recv_sem=recv_sem.at[slot], device_id=where, device_id_type=MESH,
        )

    first, last = pl.ds(reach, reach), pl.ds(height, reach)
    above, middle, below = pl.ds(0, reach), pl.ds(reach, height), pl.ds(reach + height, reach)
    quot_at, gedge_at = 8, 8 + 2 * views
    to_up = [remote(ext.at[first], ext.at[below], 0, up)] + [
        remote(quot.at[v, first], quot.at[v, below], quot_at + v, up) for v in range(views)
    ]
    to_down = [remote(ext.at[last], ext.at[above], 1, down)] + [
        remote(quot.at[v, last], quot.at[v, above], quot_at + views + v, down) for v in range(views)
    ]
    to_left = [remote(edge.at[middle], edge_r.at[middle], 2, left)] + [
        remote(gedge.at[v], gedge_r.at[v], gedge_at + v, left) for v in range(views)
    ]
    to_right = [remote(edge.at[middle], edge_l.at[middle], 3, right)] + [
        remote(gedge.at[v], gedge_l.at[v], gedge_at + views + v, right) for v in range(views)
    ]
    to_corner = [
        remote(edge.at[first], edge_r.at[below], 4, corners[0][1]),
        remote(edge.at[first], edge_l.at[below], 5, corners[1][1]),
        remote(edge.at[last], edge_r.at[above], 6, corners[2][1]),
        remote(edge.at[last], edge_l.at[above], 7, corners[3][1]),
    ]

    def start(which):
        for has, copies in which:
            @pl.when(has)
            def _(copies=copies):
                copies.start()

    def arrive(which):
        for has, copies in which:
            @pl.when(has)
            def _(copies=copies):
                copies.wait_recv()

    lane = lax.broadcasted_iota(jnp.int32, (8, width), 1)
    slot_of = ((lane + reach) // (2 * reach)) % per
    from_right = (lane // reach) % 2 == 0

    def mask(m, rows):
        return jnp.broadcast_to(m[:1], (rows, width))

    def pack(tiles):
        rows = tiles[0].shape[0]
        total = tiles[0]
        for k in range(1, per):
            total = jnp.where(mask(slot_of, rows) == k, pltpu.roll(tiles[k], 2 * reach * k, 1), total)
        return total.astype(BF)

    def unpack(tile, k):
        return tile if k == 0 else pltpu.roll(tile, width - 2 * reach * k, 1)

    local[0].wait()
    for p in range(planes):
        ext[middle, p * width:(p + 1) * width] = est_v[p].astype(BF)
    for g in range(groups):
        edge[middle, g * width:(g + 1) * width] = pack([est_v[g * per + k] for k in range(per)])
    peers = 0
    for has, where in sides:
        peers = peers + has.astype(jnp.int32)
    pl.semaphore_wait(barrier, peers)
    start(((has_up, to_up[0]), (has_down, to_down[0])))
    start([(has, copy) for (has, _), copy in zip(corners, to_corner)])
    start(((has_left, to_left[0]), (has_right, to_right[0])))

    def clear(has, refs):
        @pl.when(jnp.logical_not(has))
        def _():
            for ref in refs:
                ref[...] = jnp.zeros(ref.shape, ref.dtype)

    clear(has_up, [ext.at[above]] + [quot.at[v, above] for v in range(views)])
    clear(has_down, [ext.at[below]] + [quot.at[v, below] for v in range(views)])
    clear(has_left, [edge_l.at[middle], gedge_l])
    clear(has_right, [edge_r.at[middle], gedge_r])
    for (has, _), ref in zip(
        corners, (edge_l.at[above], edge_r.at[above], edge_l.at[below], edge_r.at[below])
    ):
        clear(has, [ref])

    local[1].wait()
    local[2].wait()
    kp[...] = jnp.zeros(kp.shape, F32)
    psf_y, psf_x = pr_v[...], pc_v[...]
    kp[0:views, 0:taps] = psf_y / jnp.sum(psf_y, axis=1, keepdims=True)
    kp[views:2 * views, 0:taps] = psf_x / jnp.sum(psf_x, axis=1, keepdims=True)
    square = (width, width)
    apart = lax.broadcasted_iota(jnp.int32, square, 1) - lax.broadcasted_iota(jnp.int32, square, 0)
    near = (apart <= reach) & (apart >= -reach)
    for v in range(views):
        rows_y = jnp.broadcast_to(kp[v:v + 1, :], square)
        by = pltpu.roll(rows_y, 0, 1, stride=1, stride_axis=0)
        ky_s[v * height:(v + 1) * height, :] = by[:height, :inner].astype(BF)
        kt_s[v] = by.T[2 * reach:2 * reach + height, :inner].astype(BF)
        rows_x = jnp.broadcast_to(kp[views + v:views + v + 1, :], square)
        bx = pltpu.roll(rows_x, width - reach, 1, stride=1, stride_axis=0)
        core = jnp.where(near, bx, 0.0).astype(BF)
        off = jnp.where(near, 0.0, bx).astype(BF)
        df_s[v, :, :width] = core
        df_s[v, :, width:] = off
        da_s[v, :width, :] = core
        da_s[v, width:, :] = off

    arrive(((has_up, to_down[0]), (has_down, to_up[0])))
    ybuf[...] = dot(ky_s[...], ext[...]).astype(BF)
    arrive(((has_left, to_right[0]), (has_right, to_left[0])))
    arrive([(has, copy) for (has, _), copy in zip(corners, reversed(to_corner))])
    sel = jnp.concatenate([mask(from_right, inner)] * groups, axis=1)
    edges = jnp.where(sel, edge_r[...].astype(F32), edge_l[...].astype(F32)).astype(BF)
    y_edges = dot(ky_s[...], edges)

    local[3].wait()
    for v in range(views):
        vs = slice(v * height, (v + 1) * height)
        parts = []
        for p in range(planes):
            g, k = divmod(p, per)
            halo = unpack(y_edges[vs, g * width:(g + 1) * width], k).astype(BF)
            parts.append(jnp.concatenate([ybuf[vs, p * width:(p + 1) * width], halo], axis=1))
        blurred = dot(jnp.concatenate(parts, axis=0), df_s[v], 1)
        for p in range(planes):
            ratio = views_v[v, p].astype(F32) / blurred[p * height:(p + 1) * height]
            quot[v, middle, p * width:(p + 1) * width] = ratio.astype(BF)
        start(((has_up, to_up[1 + v]), (has_down, to_down[1 + v])))

    for v in range(views):
        arrive(((has_up, to_down[1 + v]), (has_down, to_up[1 + v])))
        g_v = dot(kt_s[v], quot[v])
        gbuf[v] = g_v
        for g in range(groups):
            tiles = [g_v[:, (g * per + k) * width:(g * per + k + 1) * width] for k in range(per)]
            gedge[v, :, g * width:(g + 1) * width] = pack(tiles)
        start(((has_left, to_left[1 + v]), (has_right, to_right[1 + v])))

    sel = jnp.concatenate([mask(from_right, height)] * groups, axis=1)
    product = None
    for v in range(views):
        arrive(((has_left, to_right[1 + v]), (has_right, to_left[1 + v])))
        halo = jnp.where(sel, gedge_r[v].astype(F32), gedge_l[v].astype(F32))
        parts, rest = [], []
        for p in range(planes):
            g, k = divmod(p, per)
            own = gbuf[v, :, p * width:(p + 1) * width]
            high = own.astype(BF)
            rest.append((own - high.astype(F32)).astype(BF))
            side = unpack(halo[:, g * width:(g + 1) * width], k).astype(BF)
            parts.append(jnp.concatenate([high, side], axis=1))
        corr = dot(jnp.concatenate(parts, axis=0), da_s[v])
        corr = corr + dot(jnp.concatenate(rest, axis=0), da_s[v, :width, :])
        product = corr if product is None else product * corr
    out_ref[...] = est_v[...] * jnp.sqrt(jnp.sqrt(product)).reshape(planes, height, width)

    ends = ((has_up, to_up), (has_down, to_down), (has_left, to_left), (has_right, to_right))
    for has, copies in ends + tuple((has, [copy]) for (has, _), copy in zip(corners, to_corner)):
        @pl.when(has)
        def _(copies=copies):
            for copy in copies:
                copy.wait_send()


def local_step(nr, nc, estimate, views_data, psf_rows, psf_cols):
    views, planes, height, width = views_data.shape
    taps = psf_rows.shape[1]
    reach = (taps - 1) // 2
    inner = height + 2 * reach
    per = width // (2 * reach)
    groups = planes // per
    vm = pltpu.VMEM
    any_spec = pl.BlockSpec(memory_space=pl.ANY)
    return pl.pallas_call(
        functools.partial(kernel, nr, nc, reach),
        out_shape=jax.ShapeDtypeStruct((planes, height, width), F32),
        in_specs=[any_spec] * 4,
        out_specs=pl.BlockSpec(memory_space=pltpu.VMEM),
        scratch_shapes=[
            vm((planes, height, width), F32),
            vm((views, planes, height, width), BF),
            vm((views, taps), F32),
            vm((views, taps), F32),
            vm((2 * views, width), F32),
            vm((views * height, inner), BF),
            vm((views, height, inner), BF),
            vm((views, width, 2 * width), BF),
            vm((views, 2 * width, width), BF),
            vm((inner, planes * width), BF),
            vm((views * height, planes * width), BF),
            vm((views, inner, planes * width), BF),
            vm((inner, groups * width), BF),
            vm((inner, groups * width), BF),
            vm((inner, groups * width), BF),
            vm((views, height, planes * width), F32),
            vm((views, height, groups * width), BF),
            vm((views, height, groups * width), BF),
            vm((views, height, groups * width), BF),
            pltpu.SemaphoreType.DMA((4,)),
            pltpu.SemaphoreType.DMA((8 + 4 * views,)),
            pltpu.SemaphoreType.DMA((8 + 4 * views,)),
        ],
        compiler_params=pltpu.CompilerParams(collective_id=0, has_side_effects=True),
        name="deconvolve",
    )(estimate, views_data, psf_rows, psf_cols)


def solution(mesh):
    nr, nc = mesh.shape["row"], mesh.shape["col"]
    return jax.shard_map(
        functools.partial(local_step, nr, nc),
        mesh=mesh,
        in_specs=(P(None, "row", "col"), P(None, None, "row", "col"), P(), P()),
        out_specs=P(None, "row", "col"),
        check_vma=False,
    )
```

time: 21.2 us -> 20 us (0.943)
  local copies, waits for them, and re-layouts: 3.22 us -> 1.57 us
  Pallas kernels: 17 us -> 18.3 us
  other arithmetic: 0.73 us -> 0 us
    unnamed x8 -> x1, local copies, waits for them, and re-layouts: 3.22 us -> 1.57 us
    pallas_call x1, Pallas kernels: 17 us -> 18.3 us  [local_step(): pl.pallas_call(functools.partial(kernel, nr, nc, reach), out_shape=jax.Sh...]
    mul x1 -> x0, other arithmetic: 0.73 us -> none  [local_step(): return estimate * jnp.sqrt(jnp.sqrt(product))]
where the time goes in v6:
time: 20 us; the launch traced here: 19.9 us
  Pallas kernels  18.3 us (92%)
  local copies, waits for them, and re-layouts  1.57 us (8%)
    pallas_call x1, Pallas kernels, local_step(): pl.pallas_call(functools.partial(kernel, nr, nc, reach), out_shape=jax.Sh...  18.3 us
    unnamed x1, local copies, waits for them, and re-layouts  1.57 us

profile of v6, /device:TPU:9, one launch (start us, length us, event | category | flops | bytes accessed | tf_op | source)
XLA Modules:
  0.0 19.9 jit_solution(9639039915953988716)
XLA Ops:
  0.0 18.3 %deconvolve.1 = f32[8,32,128]{2,1,0:T(8,128)} custom-call(f32[8,32,128]{2,1,0:T(8,128)} %est_hbm.1, bf16[4,8,32,128]{3,2,1,0:T(8,128)(2,1)} %views_hbm.1, f32[4,33]{1,0:T(4,128)} %pr_hbm.1, f32[4,33]{1,0:T(4,128)} %pc_hbm.1), custom_call_target="tpu_custom_call" | custom-call | tf_op jit(solution)/shard_map/deconvolve/pallas_call | solution.py:232
  18.3 1.6 %copy.6 = f32[8,32,128]{2,1,0:T(8,128)} copy(f32[8,32,128]{2,1,0:T(8,128)} %deconvolve.1) | data formatting | bytes 262144

commit v7 on v6

--- a/solution.py
+++ b/solution.py
@@ -20,13 +20,12 @@
 
 def kernel(
     nr, nc, reach,
-    est_hbm, views_hbm, pr_hbm, pc_hbm, out_ref,
-    est_v, views_v, pr_v, pc_v, kp, ky_s, kt_s, df_s, da_s,
+    est_hbm, views_hbm, psf, out_ref,
+    est_v, views_v, ky_s, kt_s, df_s, da_s,
     ext, ybuf, quot, edge, edge_l, edge_r, gbuf, gedge, gedge_l, gedge_r,
     local_sem, send_sem, recv_sem,
 ):
     views, planes, height, width = views_v.shape
-    taps = pr_v.shape[1]
     inner = height + 2 * reach
     per = width // (2 * reach)
     groups = planes // per
@@ -42,9 +41,7 @@
 
     local = [
         pltpu.make_async_copy(s, d, local_sem.at[i])
-        for i, (s, d) in enumerate(
-            ((est_hbm, est_v), (pr_hbm, pr_v), (pc_hbm, pc_v), (views_hbm, views_v))
-        )
+        for i, (s, d) in enumerate(((est_hbm, est_v), (views_hbm, views_v)))
     ]
     for copy in local:
         copy.start()
@@ -140,21 +137,16 @@
     ):
         clear(has, [ref])
 
-    local[1].wait()
-    local[2].wait()
-    kp[...] = jnp.zeros(kp.shape, F32)
-    psf_y, psf_x = pr_v[...], pc_v[...]
-    kp[0:views, 0:taps] = psf_y / jnp.sum(psf_y, axis=1, keepdims=True)
-    kp[views:2 * views, 0:taps] = psf_x / jnp.sum(psf_x, axis=1, keepdims=True)
+    taps = psf[...] / jnp.sum(psf[...], axis=1, keepdims=True)
     square = (width, width)
     apart = lax.broadcasted_iota(jnp.int32, square, 1) - lax.broadcasted_iota(jnp.int32, square, 0)
     near = (apart <= reach) & (apart >= -reach)
     for v in range(views):
-        rows_y = jnp.broadcast_to(kp[v:v + 1, :], square)
+        rows_y = jnp.broadcast_to(taps[v:v + 1], square)
         by = pltpu.roll(rows_y, 0, 1, stride=1, stride_axis=0)
         ky_s[v * height:(v + 1) * height, :] = by[:height, :inner].astype(BF)
         kt_s[v] = by.T[2 * reach:2 * reach + height, :inner].astype(BF)
-        rows_x = jnp.broadcast_to(kp[views + v:views + v + 1, :], square)
+        rows_x = jnp.broadcast_to(taps[views + v:views + v + 1], square)
         bx = pltpu.roll(rows_x, width - reach, 1, stride=1, stride_axis=0)
         core = jnp.where(near, bx, 0.0).astype(BF)
         off = jnp.where(near, 0.0, bx).astype(BF)
@@ -171,7 +163,7 @@
     edges = jnp.where(sel, edge_r[...].astype(F32), edge_l[...].astype(F32)).astype(BF)
     y_edges = dot(ky_s[...], edges)
 
-    local[3].wait()
+    local[1].wait()
     for v in range(views):
         vs = slice(v * height, (v + 1) * height)
         parts = []
@@ -227,19 +219,18 @@
     inner = height + 2 * reach
     per = width // (2 * reach)
     groups = planes // per
+    psf = jnp.concatenate([psf_rows, psf_cols])
+    psf = jnp.pad(psf, ((0, 0), (0, width - taps)))
     vm = pltpu.VMEM
     any_spec = pl.BlockSpec(memory_space=pl.ANY)
     return pl.pallas_call(
         functools.partial(kernel, nr, nc, reach),
         out_shape=jax.ShapeDtypeStruct((planes, height, width), F32),
-        in_specs=[any_spec] * 4,
+        in_specs=[any_spec] * 2 + [pl.BlockSpec(memory_space=pltpu.VMEM)],
         out_specs=pl.BlockSpec(memory_space=pltpu.VMEM),
         scratch_shapes=[
             vm((planes, height, width), F32),
             vm((views, planes, height, width), BF),
-            vm((views, taps), F32),
-            vm((views, taps), F32),
-            vm((2 * views, width), F32),
             vm((views * height, inner), BF),
             vm((views, height, inner), BF),
             vm((views, width, 2 * width), BF),
@@ -254,13 +245,15 @@
             vm((views, height, groups * width), BF),
             vm((views, height, groups * width), BF),
             vm((views, height, groups * width), BF),
-            pltpu.SemaphoreType.DMA((4,)),
+            pltpu.SemaphoreType.DMA((2,)),
             pltpu.SemaphoreType.DMA((8 + 4 * views,)),
             pltpu.SemaphoreType.DMA((8 + 4 * views,)),
         ],
-        compiler_params=pltpu.CompilerParams(collective_id=0, has_side_effects=True),
+        compiler_params=pltpu.CompilerParams(
+            collective_id=0, has_side_effects=True, vmem_limit_bytes=55036 * 1024
+        ),
         name="deconvolve",
-    )(estimate, views_data, psf_rows, psf_cols)
+    )(estimate, views_data, psf)
 
 
 def solution(mesh):

time: 20 us -> 19.2 us (0.960)
  local copies, waits for them, and re-layouts: 1.57 us -> 0.66 us
  other arithmetic: 0 us -> 0.71 us
  Pallas kernels: 18.3 us -> 17.7 us
    unnamed x1, local copies, waits for them, and re-layouts: 1.57 us -> 0.66 us
    concatenate x0 -> x1, other arithmetic: none -> 0.71 us  [local_step(): psf = jnp.concatenate([psf_rows, psf_cols])]
    pallas_call x1, Pallas kernels: 18.3 us -> 17.7 us  [local_step(): pl.pallas_call(functools.partial(kernel, nr, nc, reach), out_shape=jax.Sh...]
where the time goes in v7:
time: 19.2 us; the launch traced here: 19.1 us
  Pallas kernels  17.7 us (92%)
  other arithmetic  0.71 us (4%)
  local copies, waits for them, and re-layouts  0.66 us (3%)
    pallas_call x1, Pallas kernels, local_step(): pl.pallas_call(functools.partial(kernel, nr, nc, reach), out_shape=jax.Sh...  17.7 us
    concatenate x1, other arithmetic, local_step(): psf = jnp.concatenate([psf_rows, psf_cols])  0.71 us
    unnamed x1, local copies, waits for them, and re-layouts  0.66 us

profile of v7, /device:TPU:9, one launch (start us, length us, event | category | flops | bytes accessed | tf_op | source)
XLA Modules:
  0.0 19.1 jit_solution(8632157684991979493)
XLA Ops:
  0.0 0.7 %select_maximum_fusion.psf = f32[8,128]{1,0:T(8,128)S(1)} fusion(f32[4,33]{1,0:T(4,128)} %param.7, f32[4,33]{1,0:T(4,128)} %param.6), kind=kLoop, calls=%fused_computation | loop fusion | flops 4096 | bytes 5152 | tf_op jit(solution)/shard_map/concatenate | solution.py:222
  0.7 17.7 %deconvolve.1 = f32[8,32,128]{2,1,0:T(8,128)S(1)} custom-call(f32[8,32,128]{2,1,0:T(8,128)} %est_hbm.1, bf16[4,8,32,128]{3,2,1,0:T(8,128)(2,1)} %views_hbm.1, f32[8,128]{1,0:T(8,128)S(1)} %select_maximum_fusion.psf), custom_call_target="tpu_custom_call" | custom-call | tf_op jit(solution)/shard_map/deconvolve/pallas_call | solution.py:226
  18.4 0.7 %copy.6 = f32[8,32,128]{2,1,0:T(8,128)} copy(f32[8,32,128]{2,1,0:T(8,128)S(1)} %deconvolve.1) | data formatting | bytes 262144

commit v8 on v7

v8 whole, which is shorter than its diff:
```python
import functools

import jax
import jax.numpy as jnp
from jax import lax
from jax.experimental import pallas as pl
from jax.experimental.pallas import tpu as pltpu
from jax.sharding import PartitionSpec as P

BF = jnp.bfloat16
F32 = jnp.float32
MESH = pl.DeviceIdType.MESH


def dot(a, b, contract_b=0):
    return lax.dot_general(
        a, b, (((1,), (contract_b,)), ((), ())), preferred_element_type=F32
    )


def kernel(
    nr, nc, reach,
    est_hbm, views_hbm, psf, out_ref,
    est_v, views_v, ky_s, kt_s, df_s, da_s,
    ext, ybuf, quot, edge, side, qedge, qside,
    local_sem, send_sem, recv_sem,
):
    views, planes, height, width = views_v.shape
    inner = height + 2 * reach
    r, c = lax.axis_index("row"), lax.axis_index("col")
    up, down = (r - 1, c), (r + 1, c)
    left, right = (r, c - 1), (r, c + 1)
    has_up, has_down, has_left, has_right = r > 0, r < nr - 1, c > 0, c < nc - 1
    corners = (
        (has_up & has_left, (r - 1, c - 1)), (has_up & has_right, (r - 1, c + 1)),
        (has_down & has_left, (r + 1, c - 1)), (has_down & has_right, (r + 1, c + 1)),
    )
    sides = ((has_up, up), (has_down, down), (has_left, left), (has_right, right)) + corners

    local = [
        pltpu.make_async_copy(s, d, local_sem.at[i])
        for i, (s, d) in enumerate(((est_hbm, est_v), (views_hbm, views_v)))
    ]
    for copy in local:
        copy.start()

    barrier = pltpu.get_barrier_semaphore()
    for has, where in sides:
        @pl.when(has)
        def _():
            pl.semaphore_signal(barrier, inc=1, device_id=where, device_id_type=MESH)

    def remote(src, dst, slot, where):
        return pltpu.make_async_remote_copy(
            src_ref=src, dst_ref=dst, send_sem=send_sem.at[slot],
            recv_sem=recv_sem.at[slot], device_id=where, device_id_type=MESH,
        )

    first, last = pl.ds(reach, reach), pl.ds(height, reach)
    above, middle, below = pl.ds(0, reach), pl.ds(reach, height), pl.ds(reach + height, reach)
    quot_at, edge_at, pairs = 8, 8 + 2 * views, views // 2
    to_up = [remote(ext.at[first], ext.at[below], 0, up)] + [
        remote(quot.at[v, first], quot.at[v, below], quot_at + v, up) for v in range(views)
    ]
    to_down = [remote(ext.at[last], ext.at[above], 1, down)] + [
        remote(quot.at[v, last], quot.at[v, above], quot_at + views + v, down) for v in range(views)
    ]
    ways = (
        (0, middle, middle, has_left, left), (1, middle, middle, has_right, right),
        (0, first, below) + corners[0], (1, first, below) + corners[1],
        (0, last, above) + corners[2], (1, last, above) + corners[3],
    )
    opposite = (1, 0, 5, 4, 3, 2)
    est_ways = [
        (has, remote(edge.at[s, src], side.at[s, dst], 2 + i, where))
        for i, (s, src, dst, has, where) in enumerate(ways)
    ]
    quot_ways = [
        [
            (has, remote(
                qedge.at[s, pl.ds(2 * k, 2), src], qside.at[s, pl.ds(2 * k, 2), dst],
                edge_at + 6 * k + i, where,
            ))
            for i, (s, src, dst, has, where) in enumerate(ways)
        ]
        for k in range(pairs)
    ]

    def start(which):
        for has, copies in which:
            @pl.when(has)
            def _(copies=copies):
                copies.start()

    def arrive_edges(sent):
        arrive([(ways[j][3], sent[i][1]) for i, j in enumerate(opposite)])

    def arrive(which):
        for has, copies in which:
            @pl.when(has)
            def _(copies=copies):
                copies.wait_recv()

    lane = lax.broadcasted_iota(jnp.int32, (8, width), 1)
    group = lane // reach
    near_right = lane < width // 2

    def mask(m, rows):
        return jnp.broadcast_to(m[:1], (rows, width))

    def pack(tiles):
        rows = tiles[0].shape[0]
        turned = [t if k == 0 else pltpu.roll(t, reach * k, 1) for k, t in enumerate(tiles)]
        here, there = turned[0], turned[0]
        for k in range(1, planes):
            here = jnp.where(mask(group, rows) == k, turned[k], here)
            there = jnp.where(mask(group, rows) == k - 1, turned[k], there)
        return here.astype(BF), there.astype(BF)

    def unpack(edges, k):
        rows = edges.shape[0]
        tiles = (edges[:, :width], edges[:, width:])
        if k:
            tiles = [pltpu.roll(t, width - reach * k, 1) for t in tiles]
        return jnp.where(mask(near_right, rows), tiles[0], tiles[1]).astype(BF)

    local[0].wait()
    for p in range(planes):
        ext[middle, p * width:(p + 1) * width] = est_v[p].astype(BF)
    here, there = pack([est_v[p] for p in range(planes)])
    edge[0, middle], edge[1, middle] = here, there
    peers = 0
    for has, where in sides:
        peers = peers + has.astype(jnp.int32)
    pl.semaphore_wait(barrier, peers)
    start(((has_up, to_up[0]), (has_down, to_down[0])))
    start(est_ways)

    def clear(has, refs):
        @pl.when(jnp.logical_not(has))
        def _():
            for ref in refs:
                ref[...] = jnp.zeros(ref.shape, ref.dtype)

    clear(has_up, [ext.at[above]] + [quot.at[v, above] for v in range(views)])
    clear(has_down, [ext.at[below]] + [quot.at[v, below] for v in range(views)])
    for i, j in enumerate(opposite):
        s, _, dst, _, _ = ways[i]
        clear(ways[j][3], [side.at[s, dst]] + [qside.at[s, v, dst] for v in range(views)])

    taps = psf[...] / jnp.sum(psf[...], axis=1, keepdims=True)
    square = (width, width)
    apart = lax.broadcasted_iota(jnp.int32, square, 1) - lax.broadcasted_iota(jnp.int32, square, 0)
    near = (apart <= reach) & (apart >= -reach)
    for v in range(views):
        rows_y = jnp.broadcast_to(taps[v:v + 1], square)
        by = pltpu.roll(rows_y, 0, 1, stride=1, stride_axis=0)
        ky_s[v * height:(v + 1) * height, :] = by[:height, :inner].astype(BF)
        kt_s[v] = by.T[2 * reach:2 * reach + height, :inner].astype(BF)
        rows_x = jnp.broadcast_to(taps[views + v:views + v + 1], square)
        bx = pltpu.roll(rows_x, width - reach, 1, stride=1, stride_axis=0)
        core = jnp.where(near, bx, 0.0).astype(BF)
        off = jnp.where(near, 0.0, bx).astype(BF)
        df_s[v, :, :width] = core
        df_s[v, :, width:] = off
        da_s[v, :width, :] = core
        da_s[v, width:, :] = off

    arrive(((has_up, to_down[0]), (has_down, to_up[0])))
    ybuf[...] = dot(ky_s[...], ext[...]).astype(BF)
    arrive_edges(est_ways)
    y_edges = dot(ky_s[...], jnp.concatenate([side[0], side[1]], axis=1))

    local[1].wait()
    for v in range(views):
        vs = slice(v * height, (v + 1) * height)
        parts = []
        for p in range(planes):
            halo = unpack(y_edges[vs], p)
            parts.append(jnp.concatenate([ybuf[vs, p * width:(p + 1) * width], halo], axis=1))
        blurred = dot(jnp.concatenate(parts, axis=0), df_s[v], 1)
        ratios = [
            views_v[v, p].astype(F32) / blurred[p * height:(p + 1) * height] for p in range(planes)
        ]
        for p in range(planes):
            quot[v, middle, p * width:(p + 1) * width] = ratios[p].astype(BF)
        if v % 2 == 0:
            start(((has_up, to_up[1 + v]), (has_down, to_down[1 + v])))
        qedge[0, v, middle], qedge[1, v, middle] = pack(ratios)
        if v % 2 == 1:
            start(quot_ways[v // 2])
            start(((has_up, to_up[1 + v]), (has_down, to_down[1 + v])))

    product = None
    for v in range(views):
        arrive(((has_up, to_down[1 + v]), (has_down, to_up[1 + v])))
        g_own = dot(kt_s[v], quot[v])
        if v % 2 == 0:
            arrive_edges(quot_ways[v // 2])
        g_edges = dot(kt_s[v], jnp.concatenate([qside[0, v], qside[1, v]], axis=1))
        parts, rest = [], []
        for p in range(planes):
            own = g_own[:, p * width:(p + 1) * width]
            high = own.astype(BF)
            rest.append((own - high.astype(F32)).astype(BF))
            parts.append(jnp.concatenate([high, unpack(g_edges, p)], axis=1))
        corr = dot(jnp.concatenate(parts, axis=0), da_s[v])
        corr = corr + dot(jnp.concatenate(rest, axis=0), da_s[v, :width, :])
        product = corr if product is None else product * corr
    out_ref[...] = est_v[...] * jnp.sqrt(jnp.sqrt(product)).reshape(planes, height, width)

    sent = [(has_up, to_up), (has_down, to_down)]
    sent += [(has, [copy]) for some in [est_ways] + quot_ways for has, copy in some]
    for has, copies in sent:
        @pl.when(has)
        def _(copies=copies):
            for copy in copies:
                copy.wait_send()


def local_step(nr, nc, estimate, views_data, psf_rows, psf_cols):
    views, planes, height, width = views_data.shape
    taps = psf_rows.shape[1]
    reach = (taps - 1) // 2
    inner = height + 2 * reach
    psf = jnp.concatenate([psf_rows, psf_cols])
    psf = jnp.pad(psf, ((0, 0), (0, width - taps)))
    vm = pltpu.VMEM
    any_spec = pl.BlockSpec(memory_space=pl.ANY)
    return pl.pallas_call(
        functools.partial(kernel, nr, nc, reach),
        out_shape=jax.ShapeDtypeStruct((planes, height, width), F32),
        in_specs=[any_spec] * 2 + [pl.BlockSpec(memory_space=pltpu.VMEM)],
        out_specs=pl.BlockSpec(memory_space=pltpu.VMEM),
        scratch_shapes=[
            vm((planes, height, width), F32),
            vm((views, planes, height, width), BF),
            vm((views * height, inner), BF),
            vm((views, height, inner), BF),
            vm((views, width, 2 * width), BF),
            vm((views, 2 * width, width), BF),
            vm((inner, planes * width), BF),
            vm((views * height, planes * width), BF),
            vm((views, inner, planes * width), BF),
            vm((2, inner, width), BF),
            vm((2, inner, width), BF),
            vm((2, views, inner, width), BF),
            vm((2, views, inner, width), BF),
            pltpu.SemaphoreType.DMA((2,)),
            pltpu.SemaphoreType.DMA((8 + 5 * views,)),
            pltpu.SemaphoreType.DMA((8 + 5 * views,)),
        ],
        compiler_params=pltpu.CompilerParams(
            collective_id=0, has_side_effects=True, vmem_limit_bytes=55036 * 1024
        ),
        name="deconvolve",
    )(estimate, views_data, psf)


def solution(mesh):
    nr, nc = mesh.shape["row"], mesh.shape["col"]
    return jax.shard_map(
        functools.partial(local_step, nr, nc),
        mesh=mesh,
        in_specs=(P(None, "row", "col"), P(None, None, "row", "col"), P(), P()),
        out_specs=P(None, "row", "col"),
        check_vma=False,
    )
```

time: 19.2 us -> 17.8 us (0.927)
  Pallas kernels: 17.7 us -> 16.2 us
    pallas_call x1, Pallas kernels: 17.7 us -> 16.2 us  [local_step(): pl.pallas_call(functools.partial(kernel, nr, nc, reach), out_shape=jax.Sh...]
where the time goes in v8:
time: 17.8 us; the launch traced here: 17.6 us
  Pallas kernels  16.2 us (91%)
  other arithmetic  0.71 us (4%)
  local copies, waits for them, and re-layouts  0.66 us (4%)
    pallas_call x1, Pallas kernels, local_step(): pl.pallas_call(functools.partial(kernel, nr, nc, reach), out_shape=jax.Sh...  16.2 us
    concatenate x1, other arithmetic, local_step(): psf = jnp.concatenate([psf_rows, psf_cols])  0.71 us
    unnamed x1, local copies, waits for them, and re-layouts  0.66 us

profile of v8, /device:TPU:9, one launch (start us, length us, event | category | flops | bytes accessed | tf_op | source)
XLA Modules:
  0.0 17.6 jit_solution(16304881795168730711)
XLA Ops:
  0.0 0.7 %select_maximum_fusion.psf = f32[8,128]{1,0:T(8,128)S(1)} fusion(f32[4,33]{1,0:T(4,128)} %param.7, f32[4,33]{1,0:T(4,128)} %param.6), kind=kLoop, calls=%fused_computation | loop fusion | flops 4096 | bytes 5152 | tf_op jit(solution)/shard_map/concatenate | solution.py:226
  0.7 16.2 %deconvolve.1 = f32[8,32,128]{2,1,0:T(8,128)S(1)} custom-call(f32[8,32,128]{2,1,0:T(8,128)} %est_hbm.1, bf16[4,8,32,128]{3,2,1,0:T(8,128)(2,1)} %views_hbm.1, f32[8,128]{1,0:T(8,128)S(1)} %select_maximum_fusion.psf), custom_call_target="tpu_custom_call" | custom-call | tf_op jit(solution)/shard_map/deconvolve/pallas_call | solution.py:230
  16.9 0.7 %copy.6 = f32[8,32,128]{2,1,0:T(8,128)} copy(f32[8,32,128]{2,1,0:T(8,128)S(1)} %deconvolve.1) | data formatting | bytes 262144

commit v9 on v8

--- a/solution.py
+++ b/solution.py
@@ -164,7 +164,8 @@
         df_s[v, :, :width] = core
         df_s[v, :, width:] = off
         da_s[v, :width, :] = core
-        da_s[v, width:, :] = off
+        da_s[v, width:2 * width, :] = core
+        da_s[v, 2 * width:, :] = off
 
     arrive(((has_up, to_down[0]), (has_down, to_up[0])))
     ybuf[...] = dot(ky_s[...], ext[...]).astype(BF)
@@ -193,19 +194,18 @@
 
     product = None
     for v in range(views):
-        arrive(((has_up, to_down[1 + v]), (has_down, to_up[1 + v])))
-        g_own = dot(kt_s[v], quot[v])
         if v % 2 == 0:
             arrive_edges(quot_ways[v // 2])
         g_edges = dot(kt_s[v], jnp.concatenate([qside[0, v], qside[1, v]], axis=1))
-        parts, rest = [], []
+        outer = dot(jnp.concatenate([unpack(g_edges, p) for p in range(planes)], axis=0), da_s[v, 2 * width:, :])
+        arrive(((has_up, to_down[1 + v]), (has_down, to_up[1 + v])))
+        g_own = dot(kt_s[v], quot[v])
+        parts = []
         for p in range(planes):
             own = g_own[:, p * width:(p + 1) * width]
             high = own.astype(BF)
-            rest.append((own - high.astype(F32)).astype(BF))
-            parts.append(jnp.concatenate([high, unpack(g_edges, p)], axis=1))
-        corr = dot(jnp.concatenate(parts, axis=0), da_s[v])
-        corr = corr + dot(jnp.concatenate(rest, axis=0), da_s[v, :width, :])
+            parts.append(jnp.concatenate([high, (own - high.astype(F32)).astype(BF)], axis=1))
+        corr = dot(jnp.concatenate(parts, axis=0), da_s[v, :2 * width, :]) + outer
         product = corr if product is None else product * corr
     out_ref[...] = est_v[...] * jnp.sqrt(jnp.sqrt(product)).reshape(planes, height, width)
 
@@ -238,7 +238,7 @@
             vm((views * height, inner), BF),
             vm((views, height, inner), BF),
             vm((views, width, 2 * width), BF),
-            vm((views, 2 * width, width), BF),
+            vm((views, 3 * width, width), BF),
             vm((inner, planes * width), BF),
             vm((views * height, planes * width), BF),
             vm((views, inner, planes * width), BF),

time: 17.8 us -> 18 us (1.011)
  Pallas kernels: 16.2 us -> 16.4 us
    pallas_call x1, Pallas kernels: 16.2 us -> 16.4 us  [local_step(): pl.pallas_call(functools.partial(kernel, nr, nc, reach), out_shape=jax.Sh...]
where the time goes in v9:
time: 18 us; the launch traced here: 17.8 us
  Pallas kernels  16.4 us (91%)
  other arithmetic  0.71 us (4%)
  local copies, waits for them, and re-layouts  0.66 us (4%)
    pallas_call x1, Pallas kernels, local_step(): pl.pallas_call(functools.partial(kernel, nr, nc, reach), out_shape=jax.Sh...  16.4 us
    concatenate x1, other arithmetic, local_step(): psf = jnp.concatenate([psf_rows, psf_cols])  0.71 us
    unnamed x1, local copies, waits for them, and re-layouts  0.66 us

profile of v9, /device:TPU:9, one launch (start us, length us, event | category | flops | bytes accessed | tf_op | source)
XLA Modules:
  0.0 17.8 jit_solution(14080733010381568728)
XLA Ops:
  0.0 0.7 %select_maximum_fusion.psf = f32[8,128]{1,0:T(8,128)S(1)} fusion(f32[4,33]{1,0:T(4,128)} %param.7, f32[4,33]{1,0:T(4,128)} %param.6), kind=kLoop, calls=%fused_computation | loop fusion | flops 4096 | bytes 5152 | tf_op jit(solution)/shard_map/concatenate | solution.py:226
  0.7 16.4 %deconvolve.1 = f32[8,32,128]{2,1,0:T(8,128)S(1)} custom-call(f32[8,32,128]{2,1,0:T(8,128)} %est_hbm.1, bf16[4,8,32,128]{3,2,1,0:T(8,128)(2,1)} %views_hbm.1, f32[8,128]{1,0:T(8,128)S(1)} %select_maximum_fusion.psf), custom_call_target="tpu_custom_call" | custom-call | tf_op jit(solution)/shard_map/deconvolve/pallas_call | solution.py:230
  17.1 0.7 %copy.6 = f32[8,32,128]{2,1,0:T(8,128)} copy(f32[8,32,128]{2,1,0:T(8,128)S(1)} %deconvolve.1) | data formatting | bytes 262144

commit v10 on v9

--- a/solution.py
+++ b/solution.py
@@ -21,7 +21,7 @@
 def kernel(
     nr, nc, reach,
     est_hbm, views_hbm, psf, out_ref,
-    est_v, views_v, ky_s, kt_s, df_s, da_s,
+    est_v, views_v, ky_s, kt_s, df_s,
     ext, ybuf, quot, edge, side, qedge, qside,
     local_sem, send_sem, recv_sem,
 ):
@@ -156,16 +156,12 @@
         rows_y = jnp.broadcast_to(taps[v:v + 1], square)
         by = pltpu.roll(rows_y, 0, 1, stride=1, stride_axis=0)
         ky_s[v * height:(v + 1) * height, :] = by[:height, :inner].astype(BF)
-        kt_s[v] = by.T[2 * reach:2 * reach + height, :inner].astype(BF)
         rows_x = jnp.broadcast_to(taps[views + v:views + v + 1], square)
         bx = pltpu.roll(rows_x, width - reach, 1, stride=1, stride_axis=0)
         core = jnp.where(near, bx, 0.0).astype(BF)
         off = jnp.where(near, 0.0, bx).astype(BF)
         df_s[v, :, :width] = core
         df_s[v, :, width:] = off
-        da_s[v, :width, :] = core
-        da_s[v, width:2 * width, :] = core
-        da_s[v, 2 * width:, :] = off
 
     arrive(((has_up, to_down[0]), (has_down, to_up[0])))
     ybuf[...] = dot(ky_s[...], ext[...]).astype(BF)
@@ -192,12 +188,16 @@
             start(quot_ways[v // 2])
             start(((has_up, to_up[1 + v]), (has_down, to_down[1 + v])))
 
+    for v in range(views):
+        by = pltpu.roll(jnp.broadcast_to(taps[v:v + 1], square), 0, 1, stride=1, stride_axis=0)
+        kt_s[v] = by.T[2 * reach:2 * reach + height, :inner].astype(BF)
+
     product = None
     for v in range(views):
         if v % 2 == 0:
             arrive_edges(quot_ways[v // 2])
         g_edges = dot(kt_s[v], jnp.concatenate([qside[0, v], qside[1, v]], axis=1))
-        outer = dot(jnp.concatenate([unpack(g_edges, p) for p in range(planes)], axis=0), da_s[v, 2 * width:, :])
+        outer = dot(jnp.concatenate([unpack(g_edges, p) for p in range(planes)], axis=0), df_s[v, :, width:])
         arrive(((has_up, to_down[1 + v]), (has_down, to_up[1 + v])))
         g_own = dot(kt_s[v], quot[v])
         parts = []
@@ -205,7 +205,9 @@
             own = g_own[:, p * width:(p + 1) * width]
             high = own.astype(BF)
             parts.append(jnp.concatenate([high, (own - high.astype(F32)).astype(BF)], axis=1))
-        corr = dot(jnp.concatenate(parts, axis=0), da_s[v, :2 * width, :]) + outer
+        corr = dot(
+            jnp.concatenate(parts, axis=0), jnp.concatenate([df_s[v, :, :width]] * 2, axis=0)
+        ) + outer
         product = corr if product is None else product * corr
     out_ref[...] = est_v[...] * jnp.sqrt(jnp.sqrt(product)).reshape(planes, height, width)
 
@@ -238,7 +240,6 @@
             vm((views * height, inner), BF),
             vm((views, height, inner), BF),
             vm((views, width, 2 * width), BF),
-            vm((views, 3 * width, width), BF),
             vm((inner, planes * width), BF),
             vm((views * height, planes * width), BF),
             vm((views, inner, planes * width), BF),

time: 18 us -> 18 us (level)
  no operation moved by 1% of the time
where the time goes in v10:
time: 18 us; the launch traced here: 17.8 us
  Pallas kernels  16.4 us (91%)
  other arithmetic  0.71 us (4%)
  local copies, waits for them, and re-layouts  0.66 us (4%)
    pallas_call x1, Pallas kernels, local_step(): pl.pallas_call(functools.partial(kernel, nr, nc, reach), out_shape=jax.Sh...  16.4 us
    concatenate x1, other arithmetic, local_step(): psf = jnp.concatenate([psf_rows, psf_cols])  0.71 us
    unnamed x1, local copies, waits for them, and re-layouts  0.66 us

profile of v10, /device:TPU:9, one launch (start us, length us, event | category | flops | bytes accessed | tf_op | source)
XLA Modules:
  0.0 17.8 jit_solution(16594254728086399479)
XLA Ops:
  0.0 0.7 %select_maximum_fusion.psf = f32[8,128]{1,0:T(8,128)S(1)} fusion(f32[4,33]{1,0:T(4,128)} %param.7, f32[4,33]{1,0:T(4,128)} %param.6), kind=kLoop, calls=%fused_computation | loop fusion | flops 4096 | bytes 5152 | tf_op jit(solution)/shard_map/concatenate | solution.py:228
  0.7 16.4 %deconvolve.1 = f32[8,32,128]{2,1,0:T(8,128)S(1)} custom-call(f32[8,32,128]{2,1,0:T(8,128)} %est_hbm.1, bf16[4,8,32,128]{3,2,1,0:T(8,128)(2,1)} %views_hbm.1, f32[8,128]{1,0:T(8,128)S(1)} %select_maximum_fusion.psf), custom_call_target="tpu_custom_call" | custom-call | tf_op jit(solution)/shard_map/deconvolve/pallas_call | solution.py:232
  17.1 0.7 %copy.6 = f32[8,32,128]{2,1,0:T(8,128)} copy(f32[8,32,128]{2,1,0:T(8,128)S(1)} %deconvolve.1) | data formatting | bytes 262144

commit v11 on v10

--- a/solution.py
+++ b/solution.py
@@ -22,7 +22,7 @@
     nr, nc, reach,
     est_hbm, views_hbm, psf, out_ref,
     est_v, views_v, ky_s, kt_s, df_s,
-    ext, ybuf, quot, edge, side, qedge, qside,
+    ext, ybuf, halo_s, quot, edge, side, qedge, qside,
     local_sem, send_sem, recv_sem,
 ):
     views, planes, height, width = views_v.shape
@@ -59,12 +59,22 @@
     first, last = pl.ds(reach, reach), pl.ds(height, reach)
     above, middle, below = pl.ds(0, reach), pl.ds(reach, height), pl.ds(reach + height, reach)
     quot_at, edge_at, pairs = 8, 8 + 2 * views, views // 2
+    half = planes // 2
+
+    def rows(v, which):
+        return quot.at[v, which] if v else quot.at[v, which, pl.ds(half * width, half * width)]
+
+    def early(which):
+        return quot.at[0, which, pl.ds(0, half * width)]
+
     to_up = [remote(ext.at[first], ext.at[below], 0, up)] + [
-        remote(quot.at[v, first], quot.at[v, below], quot_at + v, up) for v in range(views)
-    ]
+        remote(rows(v, first), rows(v, below), quot_at + v, up) for v in range(views)
+    ]
+    to_up.append(remote(early(first), early(below), edge_at + 6 * pairs, up))
     to_down = [remote(ext.at[last], ext.at[above], 1, down)] + [
-        remote(quot.at[v, last], quot.at[v, above], quot_at + views + v, down) for v in range(views)
-    ]
+        remote(rows(v, last), rows(v, above), quot_at + views + v, down) for v in range(views)
+    ]
+    to_down.append(remote(early(last), early(above), edge_at + 6 * pairs + 1, down))
     ways = (
         (0, middle, middle, has_left, left), (1, middle, middle, has_right, right),
         (0, first, below) + corners[0], (1, first, below) + corners[1],
@@ -133,8 +143,8 @@
     for has, where in sides:
         peers = peers + has.astype(jnp.int32)
     pl.semaphore_wait(barrier, peers)
+    start(est_ways)
     start(((has_up, to_up[0]), (has_down, to_down[0])))
-    start(est_ways)
 
     def clear(has, refs):
         @pl.when(jnp.logical_not(has))
@@ -163,24 +173,29 @@
         df_s[v, :, :width] = core
         df_s[v, :, width:] = off
 
+    arrive_edges(est_ways)
+    y_edges = dot(ky_s[...], jnp.concatenate([side[0], side[1]], axis=1))
+    for v in range(views):
+        for p in range(planes):
+            halo_s[v, p] = unpack(y_edges[v * height:(v + 1) * height], p)
     arrive(((has_up, to_down[0]), (has_down, to_up[0])))
     ybuf[...] = dot(ky_s[...], ext[...]).astype(BF)
-    arrive_edges(est_ways)
-    y_edges = dot(ky_s[...], jnp.concatenate([side[0], side[1]], axis=1))
 
     local[1].wait()
     for v in range(views):
         vs = slice(v * height, (v + 1) * height)
-        parts = []
-        for p in range(planes):
-            halo = unpack(y_edges[vs], p)
-            parts.append(jnp.concatenate([ybuf[vs, p * width:(p + 1) * width], halo], axis=1))
-        blurred = dot(jnp.concatenate(parts, axis=0), df_s[v], 1)
-        ratios = [
-            views_v[v, p].astype(F32) / blurred[p * height:(p + 1) * height] for p in range(planes)
-        ]
-        for p in range(planes):
-            quot[v, middle, p * width:(p + 1) * width] = ratios[p].astype(BF)
+        ratios = []
+        for some in (range(half), range(half, planes)) if v == 0 else (range(planes),):
+            parts = [
+                jnp.concatenate([ybuf[vs, p * width:(p + 1) * width], halo_s[v, p]], axis=1)
+                for p in some
+            ]
+            blurred = dot(jnp.concatenate(parts, axis=0), df_s[v], 1)
+            for i, p in enumerate(some):
+                ratios.append(views_v[v, p].astype(F32) / blurred[i * height:(i + 1) * height])
+                quot[v, middle, p * width:(p + 1) * width] = ratios[p].astype(BF)
+            if v == 0 and len(ratios) == half:
+                start(((has_up, to_up[1 + views]), (has_down, to_down[1 + views])))
         if v % 2 == 0:
             start(((has_up, to_up[1 + v]), (has_down, to_down[1 + v])))
         qedge[0, v, middle], qedge[1, v, middle] = pack(ratios)
@@ -199,6 +214,8 @@
         g_edges = dot(kt_s[v], jnp.concatenate([qside[0, v], qside[1, v]], axis=1))
         outer = dot(jnp.concatenate([unpack(g_edges, p) for p in range(planes)], axis=0), df_s[v, :, width:])
         arrive(((has_up, to_down[1 + v]), (has_down, to_up[1 + v])))
+        if v == 0:
+            arrive(((has_up, to_down[1 + views]), (has_down, to_up[1 + views])))
         g_own = dot(kt_s[v], quot[v])
         parts = []
         for p in range(planes):
@@ -242,14 +259,15 @@
             vm((views, width, 2 * width), BF),
             vm((inner, planes * width), BF),
             vm((views * height, planes * width), BF),
+            vm((views, planes, height, width), BF),
             vm((views, inner, planes * width), BF),
             vm((2, inner, width), BF),
             vm((2, inner, width), BF),
             vm((2, views, inner, width), BF),
             vm((2, views, inner, width), BF),
             pltpu.SemaphoreType.DMA((2,)),
-            pltpu.SemaphoreType.DMA((8 + 5 * views,)),
-            pltpu.SemaphoreType.DMA((8 + 5 * views,)),
+            pltpu.SemaphoreType.DMA((10 + 5 * views,)),
+            pltpu.SemaphoreType.DMA((10 + 5 * views,)),
         ],
         compiler_params=pltpu.CompilerParams(
             collective_id=0, has_side_effects=True, vmem_limit_bytes=55036 * 1024

time: 18 us -> 18.1 us (level)
  Pallas kernels: 16.4 us -> 16.6 us
where the time goes in v11:
time: 18.1 us; the launch traced here: 18 us
  Pallas kernels  16.6 us (92%)
  other arithmetic  0.71 us (4%)
  local copies, waits for them, and re-layouts  0.66 us (4%)
    pallas_call x1, Pallas kernels, local_step(): pl.pallas_call(functools.partial(kernel, nr, nc, reach), out_shape=jax.Sh...  16.6 us
    concatenate x1, other arithmetic, local_step(): psf = jnp.concatenate([psf_rows, psf_cols])  0.71 us
    unnamed x1, local copies, waits for them, and re-layouts  0.66 us

profile of v11, /device:TPU:9, one launch (start us, length us, event | category | flops | bytes accessed | tf_op | source)
XLA Modules:
  0.0 18.0 jit_solution(7784868629908883953)
XLA Ops:
  0.0 0.7 %select_maximum_fusion.psf = f32[8,128]{1,0:T(8,128)S(1)} fusion(f32[4,33]{1,0:T(4,128)} %param.7, f32[4,33]{1,0:T(4,128)} %param.6), kind=kLoop, calls=%fused_computation | loop fusion | flops 4096 | bytes 5152 | tf_op jit(solution)/shard_map/concatenate | solution.py:245
  0.7 16.6 %deconvolve.1 = f32[8,32,128]{2,1,0:T(8,128)S(1)} custom-call(f32[8,32,128]{2,1,0:T(8,128)} %est_hbm.1, bf16[4,8,32,128]{3,2,1,0:T(8,128)(2,1)} %views_hbm.1, f32[8,128]{1,0:T(8,128)S(1)} %select_maximum_fusion.psf), custom_call_target="tpu_custom_call" | custom-call | tf_op jit(solution)/shard_map/deconvolve/pallas_call | solution.py:249
  17.3 0.7 %copy.6 = f32[8,32,128]{2,1,0:T(8,128)} copy(f32[8,32,128]{2,1,0:T(8,128)S(1)} %deconvolve.1) | data formatting | bytes 262144

commit v12 on v8

--- a/solution.py
+++ b/solution.py
@@ -184,11 +184,12 @@
         ]
         for p in range(planes):
             quot[v, middle, p * width:(p + 1) * width] = ratios[p].astype(BF)
-        if v % 2 == 0:
+        if v < views - 1:
             start(((has_up, to_up[1 + v]), (has_down, to_down[1 + v])))
         qedge[0, v, middle], qedge[1, v, middle] = pack(ratios)
         if v % 2 == 1:
             start(quot_ways[v // 2])
+        if v == views - 1:
             start(((has_up, to_up[1 + v]), (has_down, to_down[1 + v])))
 
     product = None

time: 17.8 us -> 18 us (1.011)
  the two profiles are of different devices: /device:TPU:9 before, /device:TPU:11 now
where the time goes in v12:
time: 18 us; the launch traced here: 17.8 us
  Pallas kernels  16.5 us (92%)
  other arithmetic  0.71 us (4%)
  local copies, waits for them, and re-layouts  0.66 us (4%)
    pallas_call x1, Pallas kernels, local_step(): pl.pallas_call(functools.partial(kernel, nr, nc, reach), out_shape=jax.Sh...  16.5 us
    concatenate x1, other arithmetic, local_step(): psf = jnp.concatenate([psf_rows, psf_cols])  0.71 us
    unnamed x1, local copies, waits for them, and re-layouts  0.66 us

profile of v12, /device:TPU:11, one launch (start us, length us, event | category | flops | bytes accessed | tf_op | source)
XLA Modules:
  0.0 17.8 jit_solution(7325780958899417979)
XLA Ops:
  0.0 0.7 %select_maximum_fusion.psf = f32[8,128]{1,0:T(8,128)S(1)} fusion(f32[4,33]{1,0:T(4,128)} %param.7, f32[4,33]{1,0:T(4,128)} %param.6), kind=kLoop, calls=%fused_computation | loop fusion | flops 4096 | bytes 5152 | tf_op jit(solution)/shard_map/concatenate | solution.py:227
  0.7 16.5 %deconvolve.1 = f32[8,32,128]{2,1,0:T(8,128)S(1)} custom-call(f32[8,32,128]{2,1,0:T(8,128)} %est_hbm.1, bf16[4,8,32,128]{3,2,1,0:T(8,128)(2,1)} %views_hbm.1, f32[8,128]{1,0:T(8,128)S(1)} %select_maximum_fusion.psf), custom_call_target="tpu_custom_call" | custom-call | tf_op jit(solution)/shard_map/deconvolve/pallas_call | solution.py:231
  17.2 0.7 %copy.6 = f32[8,32,128]{2,1,0:T(8,128)} copy(f32[8,32,128]{2,1,0:T(8,128)S(1)} %deconvolve.1) | data formatting | bytes 262144
